TPU v7x, 32 devices: a whole 2x2x4 slice. The times are simulated.
32 devices in a mesh: branch: 4 (over z), ctx: 8 (over y, x, core).
Axes of the slice: x: 2, y: 2, z: 4, core: 2. Of those that a mesh axis runs over, the one named last changes fastest.
Arguments:
- summary_q: bfloat16 [16384, 2560], P(('branch', 'ctx')), may hold values from -32 to 32
- summary_kv: bfloat16 [16384, 2, 512], P(('branch', 'ctx')), may hold values from -12 to 12
- kv_cache: bfloat16 [128, 2, 128, 512], P(('branch', 'ctx')), may hold values from -9 to 9
- block_slot: int32 [128], replicated, may hold values from 0 to 127, as said below
- tile_blocks: int32 [128, 4], P(('branch', 'ctx')), may hold values from 0 to 127, as said below
- tile_count: int32 [128], P(('branch', 'ctx')), may hold values from 2 to 4
Outputs:
- attended: bfloat16 [16384, 2560], P(('branch', 'ctx'))
Inputs may be any that keep to these rules, and one draw needn't show every extreme that they name: `block_slot`: each slot number appears once; slot s lies on the device of index s // 4 along branch+ctx. `tile_blocks`: among the first tile_count[t] entries of the 4 tiles of one device, at most 2 are stored on devices of one ctx index and at most 1 on one device; entries after tile_count[t] are not read.
All inputs are finite; a program needn't handle non-finite values.
Results may differ from a plain program's by a relative error of at most 0.0045.
Values may be sent and summed in bfloat16 or wider, within the bound.
A program may use at most 192 MiB of HBM per device.

v0:
```python
import jax
import jax.numpy as jnp
from jax import lax
from jax.sharding import PartitionSpec as P

HEAD = 128
REQ_TILES = 32


def from_behind(value, axis, steps):
    count = lax.axis_size(axis)
    pairs = [(source, (source + steps) % count) for source in range(count)]
    return lax.ppermute(value, axis, pairs)


def request_table(dest_index, live_mask, count_dest, capacity, payload):
    onehot = (
        (dest_index[:, None] == jnp.arange(count_dest, dtype=jnp.int32)[None, :])
        & live_mask[:, None]
    ).astype(jnp.int32)
    rank_within = jnp.sum(onehot * (jnp.cumsum(onehot, axis=0) - 1), axis=1)
    position = dest_index * capacity + rank_within
    target = jnp.where(live_mask, position, -1)
    slot_ids = jnp.arange(count_dest * capacity, dtype=jnp.int32)
    requests = jnp.max(
        jnp.where(target[:, None] == slot_ids[None, :], payload[:, None], -1), axis=0
    )
    return (requests.reshape(count_dest, capacity), position)


def absorb(running, queries, key_rows, value_rows, key_mask, score_form, value_form, score_scale):
    old_max, old_sum, old_weighted = running
    block_scores = (
        jnp.einsum(score_form, queries, key_rows, preferred_element_type=jnp.float32) * score_scale
    )
    if key_mask is not None:
        block_scores = jnp.where(key_mask, block_scores, -jnp.inf)
    new_max = jnp.maximum(old_max, jnp.max(block_scores, axis=-1))
    block_weights = jnp.exp(block_scores - new_max[..., None])
    rescale = jnp.exp(old_max - new_max)
    new_sum = old_sum * rescale + jnp.sum(block_weights, axis=-1)
    new_weighted = old_weighted * rescale[..., None] + jnp.einsum(
        value_form,
        block_weights.astype(jnp.bfloat16),
        value_rows,
        preferred_element_type=jnp.float32,
    )
    return (new_max, new_sum, new_weighted)


def keep_state(running, earlier):
    return running


def local(summary_q, summary_kv, kv_cache, block_slot, tile_blocks, tile_count):
    shards = lax.axis_size("ctx")
    tile_num, list_len = tile_blocks.shape
    blk_dev = kv_cache.shape[0]
    block_len = kv_cache.shape[2]
    kv_width = kv_cache.shape[3]
    kv_heads = kv_width // HEAD
    rows = summary_q.shape[0]
    tile_rows = rows // tile_num
    repeat = summary_q.shape[1] // kv_width
    col_cap = max(2, -(-(tile_num * list_len) // shards))
    req_devs = REQ_TILES // tile_num
    score_scale = HEAD ** (-0.5)
    entries = tile_blocks.reshape(-1)
    live_mask = (jnp.arange(list_len, dtype=jnp.int32)[None, :] < tile_count[:, None]).reshape(-1)
    block_ids = jnp.arange(block_slot.shape[0], dtype=jnp.int32)
    stored_at = jnp.sum(
        jnp.where(entries[:, None] == block_ids[None, :], block_slot[None, :], 0), axis=1
    )
    owner_dev = stored_at // blk_dev
    local_slot = stored_at % blk_dev
    column = lax.all_gather(kv_cache, "branch", axis=0, tiled=True)
    requests, position = request_table(
        owner_dev % shards, live_mask, shards, col_cap, owner_dev // shards * blk_dev + local_slot
    )
    payload = column[
        jnp.maximum(lax.all_to_all(requests, "ctx", split_axis=0, concat_axis=0, tiled=True), 0)
    ]
    received = lax.all_to_all(payload, "ctx", split_axis=0, concat_axis=0, tiled=True)
    received = received.reshape(-1, 2, block_len, kv_width)
    position = jnp.where(live_mask, position, 0).reshape(tile_num, list_len)
    queries = summary_q.reshape(tile_num, tile_rows, kv_heads, repeat, HEAD)
    own_kv = summary_kv.reshape(rows, 2, kv_heads, HEAD)
    query_pos = jnp.arange(rows, dtype=jnp.int32).reshape(tile_num, tile_rows)
    causal = (
        query_pos[:, None, None, :, None]
        >= jnp.arange(rows, dtype=jnp.int32)[None, None, None, None, :]
    )
    scores = (
        jnp.einsum("tqgrd,kgd->tgrqk", queries, own_kv[:, 0], preferred_element_type=jnp.float32)
        * score_scale
    )
    scores = jnp.where(causal, scores, -jnp.inf)
    row_max = jnp.max(scores, axis=-1)
    weights = jnp.exp(scores - row_max[..., None])
    row_sum = jnp.sum(weights, axis=-1)
    weighted = jnp.einsum(
        "tgrqk,kgd->tgrqd",
        weights.astype(jnp.bfloat16),
        own_kv[:, 1],
        preferred_element_type=jnp.float32,
    )
    running = (row_max, row_sum, weighted)

    def take_earlier(state, earlier):
        return absorb(
            state,
            queries,
            earlier[:, 0],
            earlier[:, 1],
            None,
            "tqgrd,kgd->tgrqk",
            "tgrqk,kgd->tgrqd",
            score_scale,
        )

    flat_index = lax.axis_index("branch") * shards + lax.axis_index("ctx")
    place = (flat_index - 1 + req_devs) % req_devs
    passed = summary_kv
    for distance in range(1, req_devs):
        passed = from_behind(passed, ("branch", "ctx"), 1)
        running = lax.cond(
            place >= distance,
            take_earlier,
            keep_state,
            running,
            passed.reshape(rows, 2, kv_heads, HEAD),
        )
    pair_slots = position.reshape(tile_num, list_len // 2, 2)
    step_count = (jnp.max(tile_count) + 1) // 2

    def advance(step_idx, state):
        where_now = lax.dynamic_index_in_dim(pair_slots, step_idx, axis=1, keepdims=False)
        blocks = received[where_now]
        key_rows = blocks[:, :, 0].reshape(tile_num, 2 * block_len, kv_heads, HEAD)
        value_rows = blocks[:, :, 1].reshape(tile_num, 2 * block_len, kv_heads, HEAD)
        valid_keys = (step_idx * 2 + jnp.arange(2, dtype=jnp.int32))[None, :] < tile_count[:, None]
        valid_keys = jnp.repeat(valid_keys, block_len, axis=1)
        return absorb(
            state,
            queries,
            key_rows,
            value_rows,
            valid_keys[:, None, None, None, :],
            "tqgrd,tkgd->tgrqk",
            "tgrqk,tkgd->tgrqd",
            score_scale,
        )

    row_max, row_sum, weighted = lax.fori_loop(0, step_count, advance, running)
    result = (
        (weighted / row_sum[..., None]).transpose(0, 3, 1, 2, 4).reshape(tile_num * tile_rows, -1)
    )
    return result.astype(jnp.bfloat16)


def solution(mesh):
    in_specs = (
        P(("branch", "ctx"), None),
        P(("branch", "ctx"), None, None),
        P(("branch", "ctx"), None, None, None),
        P(),
        P(("branch", "ctx"), None),
        P(("branch", "ctx")),
    )
    out_specs = P(("branch", "ctx"), None)
    return jax.shard_map(local, mesh=mesh, in_specs=in_specs, out_specs=out_specs, check_vma=False)
```

profile of v0, /device:TPU:8, one launch (start us, length us, event | category | flops | bytes accessed | tf_op | source)
XLA Modules:
  0.0 471.7 jit_solution(16339551770722381142)
XLA Ops:
  9.8 23.5 %collective-permute-done = bf16[512,2,512]{0,2,1:T(8,128)(2,1)S(1)} collective-permute-done((bf16[512,2,512]{0,2,1:T(8,128)(2,1)S(1)}, bf16[512,2,512]{0,2,1:T(8,128)(2,1)S(1)}, u32[]{:S(2)}, u32[]{:S(2)}) %collective-permute-start) | collective-permute-done | bytes 1048608 | tf_op jit(solution)/shard_map/ppermute | solution.py:13
  33.3 38.5 %collective-permute-done.1 = bf16[512,2,512]{0,2,1:T(8,128)(2,1)S(1)} collective-permute-done((bf16[512,2,512]{0,2,1:T(8,128)(2,1)S(1)}, bf16[512,2,512]{0,2,1:T(8,128)(2,1)S(1)}, u32[]{:S(2)}, u32[]{:S(2)}) %collective-permute-start.1) | collective-permute-done | bytes 1048608 | tf_op jit(solution)/shard_map/ppermute | solution.py:13
  74.3 36.1 %collective-permute-done.2 = bf16[512,2,512]{0,2,1:T(8,128)(2,1)} collective-permute-done((bf16[512,2,512]{0,2,1:T(8,128)(2,1)S(1)}, bf16[512,2,512]{0,2,1:T(8,128)(2,1)}, u32[]{:S(2)}, u32[]{:S(2)}) %collective-permute-start.2) | collective-permute-done | bytes 1048608 | tf_op jit(solution)/shard_map/ppermute | solution.py:13
  111.4 13.7 %all-to-all-start = ((s32[8,1,2]{2,1,0:T(1,128)}), s32[8,1,2]{2,1,0:T(1,128)S(1)}, u32[]{:S(2)}, u32[]{:S(2)}) async-start(s32[8,1,2]{2,1,0:T(1,128)} %bitcast.78), calls=%async_computation | async-start | bytes 8192 | tf_op jit(solution)/shard_map/all_to_all | solution.py:81
  125.1 4.4 copy.138
  133.9 5.0 %gather_fusion.1 = bf16[16,2,128,512]{3,2,1,0:T(8,128)(2,1)} fusion(bf16[16,2,128,512]{3,2,1,0:T(8,128)(2,1)} %all-gather.2.cloned.1.call-done, s32[1024]{0:T(1024)S(1)} %pad_clamp_fusion.1), kind=kCustom, calls=%fused_computation.1 | custom fusion | bytes 8388672 | tf_op jit(solution)/shard_map/gather | solution.py:80
  138.9 6.5 %all-to-all-start.1 = ((bf16[8,2,2,128,512]{4,3,2,1,0:T(8,128)(2,1)}), bf16[8,2,2,128,512]{4,3,2,1,0:T(8,128)(2,1)}, u32[]{:S(2)}, u32[]{:S(2)}) async-start(bf16[8,2,2,128,512]{4,3,2,1,0:T(8,128)(2,1)} %bitcast.315), calls=%async_computation.1 | async-start | bytes 8388608 | tf_op jit(solution)/shard_map/all_to_all | solution.py:83
  145.4 9.8 %fusion.102 = (f32[4,4,5,128]{3,2,0,1:T(8,128)S(1)}, f32[4,512,4,128,5]{3,1,4,2,0:T(8,128)}) fusion(pred[4,128,512]{1,2,0:T(8,128)(4,1)S(1)} %iota_compare_fusion, bf16[4,128,4,5,128]{1,0,4,3,2:T(4,128)(2,1)S(1)} %reshape.233, bf16[512,2,4,128]{0,3,2,1:T(8,128)(2,1)} %bitcast.316), kind=kOutput, calls=%fused_computation.144 | convolution fusion | flops 1357895680 | bytes 24420352 | tf_op jit(solution)/shard_map/tqgrd,kgd->tgrqk/dot_general | solution.py:94
  161.3 11.6 %fusion.109 = f32[4,4,5,128,128]{4,3,2,0,1:T(8,128)} fusion(f32[4,512,4,128,5]{3,1,4,2,0:T(8,128)} %get-tuple-element.483, f32[4,4,5,128]{3,2,0,1:T(8,128)S(1)} %get-tuple-element.482, pred[4,128,512]{1,2,0:T(8,128)(4,1)S(1)} %iota_compare_fusion, bf16[512,2,4,128]{0,3,2,1:T(8,128)(2,1)} %bitcast.317), kind=kOutput, calls=%fused_computation.151 | convolution fusion | flops 1363148800 | bytes 27041792 | tf_op jit(solution)/shard_map/tgrqk,kgd->tgrqd/dot_general | solution.py:101
  172.8 4.4 collective-permute-done.5
  177.2 26.6 %collective-permute-start.6 = (bf16[512,2,512]{0,2,1:T(8,128)(2,1)}, bf16[512,2,512]{0,2,1:T(8,128)(2,1)}, u32[]{:S(2)}, u32[]{:S(2)}) collective-permute-start(bf16[512,2,512]{0,2,1:T(8,128)(2,1)} %collective-permute-done.5), channel_id=1, source_target_pairs={{0,1},{1,2},{2,3},{3,4},{4,5},{5,6},{6,7},{7,8},{8,9},{9,10},{10,1... | collective-permute-start | bytes 3145736 | tf_op jit(solution)/shard_map/ppermute | solution.py:13
  203.9 9.5 %fusion.101 = f32[4,4,5,128]{3,2,0,1:T(8,128)S(1)} fusion(f32[4,512,4,128,5]{3,1,4,2,0:T(8,128)} %get-tuple-element.483, f32[4,4,5,128]{3,2,0,1:T(8,128)S(1)} %get-tuple-element.482, pred[4,128,512]{1,2,0:T(8,128)(4,1)S(1)} %iota_compare_fusion), kind=kLoop, calls=%fused_computation.143 | loop fusion | flops 20961280 | bytes 21315584 | tf_op jit(solution)/shard_map/reduce_sum | solution.py:100
  213.4 26.7 %conditional.7 = ((f32[4,4,5,128]{3,2,0,1:T(8,128)S(1)}, f32[4,4,5,128]{3,2,0,1:T(8,128)S(1)}, f32[4,4,5,128,128]{4,3,2,0,1:T(8,128)})) conditional(s32[]{:T(128)} %convert_element_type.66, (f32[4,4,5,128]{3,2,0,1:T(8,128)S(1)}, f32[4,4,5,128]{3,2,0,1:T(8,128)S(1)}, f32[4,4,5,128,128]{4,3,2,0,1:T(8,128)}) %tuple.52, ...), branch_computations={%region_2.3_spmd, %region_3.6_spmd} | conditional | flops 2728939520 | bytes 167952480 | solution.py:126
  216.0 3.9 bitcast_reduce_fusion
  219.9 3.6 fusion.2
  223.6 3.6 copy-done.1
  227.3 12.8 %bitcast_add_fusion = f32[4,4,5,128,128]{4,3,2,0,1:T(8,128)} fusion(f32[4,4,5,128,128]{4,3,2,0,1:T(8,128)} %get-tuple-element.158, f32[4,4,5,128]{3,2,0,1:T(8,128)S(1)} %get-tuple-element.447, f32[4,512,4,128,5]{3,1,4,2,0:T(8,128)} %copy-done.1, f32[4,4,5,128]{3,2,0,1:T(8,128)S(1)} %max.27, bf16[512,2,4,128]{3,0,2,1:T(8,128)(2,1)S(1)} %copy-done.8), kind=kOutput, calls=%fused_computation.10 | convolution fusion | flops 1360527360 | bytes 32112640 | tf_op jit(solution)/shard_map/cond/branch_1_fun/tgrqk,kgd->tgrqd/dot_general | solution.py:42
  240.0 26.9 %conditional.8 = ((f32[4,4,5,128]{3,2,0,1:T(8,128)S(1)}, f32[4,4,5,128]{3,2,0,1:T(8,128)S(1)}, f32[4,4,5,128,128]{4,3,2,0,1:T(8,128)})) conditional(s32[]{:T(128)} %convert_element_type.65, (f32[4,4,5,128]{3,2,0,1:T(8,128)S(1)}, f32[4,4,5,128]{3,2,0,1:T(8,128)S(1)}, f32[4,4,5,128,128]{4,3,2,0,1:T(8,128)}) %get-tuple-element.630, ...), branch_computations={%region_6.7_spmd, %region_7.10_spmd} | conditional | flops 2728939520 | bytes 167952480 | solution.py:126
  242.9 3.9 bitcast_reduce_fusion.1
  250.5 3.6 copy-done.2
  254.2 12.8 %bitcast_add_fusion.1 = f32[4,4,5,128,128]{4,3,2,0,1:T(8,128)} fusion(f32[4,4,5,128,128]{4,3,2,0,1:T(8,128)} %get-tuple-element.163, f32[4,4,5,128]{3,2,0,1:T(8,128)S(1)} %get-tuple-element.449, f32[4,512,4,128,5]{3,1,4,2,0:T(8,128)} %copy-done.2, f32[4,4,5,128]{3,2,0,1:T(8,128)S(1)} %max.28, bf16[512,2,4,128]{3,0,2,1:T(8,128)(2,1)S(1)} %copy-done.9), kind=kOutput, calls=%fused_computation.26 | convolution fusion | flops 1360527360 | bytes 32112640 | tf_op jit(solution)/shard_map/cond/branch_1_fun/tgrqk,kgd->tgrqd/dot_general | solution.py:42
  267.0 26.6 %conditional.9 = ((f32[4,4,5,128]{3,2,0,1:T(8,128)S(1)}, f32[4,4,5,128]{3,2,0,1:T(8,128)S(1)}, f32[4,4,5,128,128]{4,3,2,0,1:T(8,128)})) conditional(s32[]{:T(128)} %convert_element_type.64, (f32[4,4,5,128]{3,2,0,1:T(8,128)S(1)}, f32[4,4,5,128]{3,2,0,1:T(8,128)S(1)}, f32[4,4,5,128,128]{4,3,2,0,1:T(8,128)}) %get-tuple-element.631, ...), branch_computations={%region_10.11_spmd, %region_11.14_spmd} | conditional | flops 2728939520 | bytes 167952480 | solution.py:126
  269.4 3.9 bitcast_reduce_fusion.2
  277.0 3.6 copy-done.3
  280.7 12.8 %bitcast_add_fusion.2 = f32[4,4,5,128,128]{4,3,2,0,1:T(8,128)} fusion(f32[4,4,5,128,128]{4,3,2,0,1:T(8,128)} %get-tuple-element.168, f32[4,4,5,128]{3,2,0,1:T(8,128)S(1)} %get-tuple-element.451, f32[4,512,4,128,5]{3,1,4,2,0:T(8,128)} %copy-done.3, f32[4,4,5,128]{3,2,0,1:T(8,128)S(1)} %max.29, bf16[512,2,4,128]{3,0,2,1:T(8,128)(2,1)S(1)} %copy-done.10), kind=kOutput, calls=%fused_computation.42 | convolution fusion | flops 1360527360 | bytes 32112640 | tf_op jit(solution)/shard_map/cond/branch_1_fun/tgrqk,kgd->tgrqd/dot_general | solution.py:42
  293.5 26.6 %conditional.10 = ((f32[4,4,5,128]{3,2,0,1:T(8,128)S(1)}, f32[4,4,5,128]{3,2,0,1:T(8,128)S(1)}, f32[4,4,5,128,128]{4,3,2,0,1:T(8,128)})) conditional(s32[]{:T(128)} %convert_element_type.63, (f32[4,4,5,128]{3,2,0,1:T(8,128)S(1)}, f32[4,4,5,128]{3,2,0,1:T(8,128)S(1)}, f32[4,4,5,128,128]{4,3,2,0,1:T(8,128)}) %get-tuple-element.632, ...), branch_computations={%region_14.15_spmd, %region_15.18_spmd} | conditional | flops 2728939520 | bytes 167952480 | solution.py:126
  296.0 3.9 bitcast_reduce_fusion.3
  300.0 3.6 fusion.38
  303.6 3.6 copy-done.4
  307.3 12.8 %bitcast_add_fusion.3 = f32[4,4,5,128,128]{4,3,2,0,1:T(8,128)} fusion(f32[4,4,5,128,128]{4,3,2,0,1:T(8,128)} %get-tuple-element.173, f32[4,4,5,128]{3,2,0,1:T(8,128)S(1)} %get-tuple-element.453, f32[4,512,4,128,5]{3,1,4,2,0:T(8,128)} %copy-done.4, f32[4,4,5,128]{3,2,0,1:T(8,128)S(1)} %max.30, bf16[512,2,4,128]{3,0,2,1:T(8,128)(2,1)S(1)} %copy-done.11), kind=kOutput, calls=%fused_computation.58 | convolution fusion | flops 1360527360 | bytes 32112640 | tf_op jit(solution)/shard_map/cond/branch_1_fun/tgrqk,kgd->tgrqd/dot_general | solution.py:42
  320.1 26.6 %conditional.11 = ((f32[4,4,5,128]{3,2,0,1:T(8,128)S(1)}, f32[4,4,5,128]{3,2,0,1:T(8,128)S(1)}, f32[4,4,5,128,128]{4,3,2,0,1:T(8,128)})) conditional(s32[]{:T(128)} %convert_element_type.62, (f32[4,4,5,128]{3,2,0,1:T(8,128)S(1)}, f32[4,4,5,128]{3,2,0,1:T(8,128)S(1)}, f32[4,4,5,128,128]{4,3,2,0,1:T(8,128)}) %get-tuple-element.633, ...), branch_computations={%region_18.19_spmd, %region_19.22_spmd} | conditional | flops 2728939520 | bytes 167952480 | solution.py:126
  322.6 3.9 bitcast_reduce_fusion.4
  330.2 3.6 copy-done.5
  333.9 12.8 %bitcast_add_fusion.4 = f32[4,4,5,128,128]{4,3,2,0,1:T(8,128)} fusion(f32[4,4,5,128,128]{4,3,2,0,1:T(8,128)} %get-tuple-element.178, f32[4,4,5,128]{3,2,0,1:T(8,128)S(1)} %get-tuple-element.455, f32[4,512,4,128,5]{3,1,4,2,0:T(8,128)} %copy-done.5, f32[4,4,5,128]{3,2,0,1:T(8,128)S(1)} %max.31, bf16[512,2,4,128]{3,0,2,1:T(8,128)(2,1)S(1)} %copy-done.12), kind=kOutput, calls=%fused_computation.74 | convolution fusion | flops 1360527360 | bytes 32112640 | tf_op jit(solution)/shard_map/cond/branch_1_fun/tgrqk,kgd->tgrqd/dot_general | solution.py:42
  346.7 26.7 %conditional.12 = ((f32[4,4,5,128]{3,2,0,1:T(8,128)S(1)}, f32[4,4,5,128]{3,2,0,1:T(8,128)S(1)}, f32[4,4,5,128,128]{4,3,2,0,1:T(8,128)})) conditional(s32[]{:T(128)} %convert_element_type.61, (f32[4,4,5,128]{3,2,0,1:T(8,128)S(1)}, f32[4,4,5,128]{3,2,0,1:T(8,128)S(1)}, f32[4,4,5,128,128]{4,3,2,0,1:T(8,128)}) %get-tuple-element.634, ...), branch_computations={%region_22.23_spmd, %region_23.26_spmd} | conditional | flops 2728939520 | bytes 167952480 | solution.py:126
  349.3 3.9 bitcast_reduce_fusion.5
  356.9 3.6 copy-done.6
  360.6 12.8 %bitcast_add_fusion.5 = f32[4,4,5,128,128]{4,3,2,0,1:T(8,128)} fusion(f32[4,4,5,128,128]{4,3,2,0,1:T(8,128)} %get-tuple-element.183, f32[4,4,5,128]{3,2,0,1:T(8,128)S(1)} %get-tuple-element.457, f32[4,512,4,128,5]{3,1,4,2,0:T(8,128)} %copy-done.6, f32[4,4,5,128]{3,2,0,1:T(8,128)S(1)} %max.32, bf16[512,2,4,128]{3,0,2,1:T(8,128)(2,1)S(1)} %copy-done.13), kind=kOutput, calls=%fused_computation.90 | convolution fusion | flops 1360527360 | bytes 32112640 | tf_op jit(solution)/shard_map/cond/branch_1_fun/tgrqk,kgd->tgrqd/dot_general | solution.py:42
  373.4 26.4 %conditional.13 = (f32[4,4,5,128]{3,2,1,0:T(8,128)S(1)}, f32[4,4,5,128]{3,2,1,0:T(8,128)S(1)}, f32[4,4,5,128,128]{4,3,2,1,0:T(8,128)}) conditional(s32[]{:T(128)} %convert_element_type.60, (f32[4,4,5,128]{3,2,0,1:T(8,128)S(1)}, f32[4,4,5,128]{3,2,0,1:T(8,128)S(1)}, f32[4,4,5,128,128]{4,3,2,0,1:T(8,128)}) %get-tuple-element.635, ...), branch_computations={%region_26.27_spmd, %region_27.30_spmd} | conditional | flops 2728939520 | bytes 172179520 | solution.py:126
  374.0 4.2 bitcast_reduce_fusion.6
  385.2 11.6 %bitcast_add_fusion.6 = f32[4,4,5,128,128]{4,3,2,0,1:T(8,128)S(1)} fusion(f32[4,4,5,128,128]{4,3,2,0,1:T(8,128)} %get-tuple-element.188, f32[4,4,5,128]{3,2,0,1:T(8,128)S(1)} %get-tuple-element.459, f32[4,512,4,128,5]{3,1,4,2,0:T(8,128)} %copy-done.7, f32[4,4,5,128]{3,2,0,1:T(8,128)S(1)} %max.33, bf16[512,2,4,128]{0,3,2,1:T(8,128)(2,1)} %bitcast.48), kind=kOutput, calls=%fused_computation.106 | convolution fusion | flops 1360527360 | bytes 32063488 | tf_op jit(solution)/shard_map/cond/branch_1_fun/tgrqk,kgd->tgrqd/dot_general | solution.py:42
  399.8 50.7 %while.14 = (s32[]{:T(128)}, f32[4,4,5,128]{3,2,1,0:T(8,128)S(1)}, f32[4,4,5,128]{3,2,1,0:T(8,128)S(1)}, f32[4,4,5,128,128]{4,3,2,1,0:T(8,128)}, s32[]{:T(128)},...) while((s32[]{:T(128)}, f32[4,4,5,128]{3,2,1,0:T(8,128)S(1)}, ...), condition=%wide.region_38.39_spmd, body=%wide.region_35.38_spmd.sunk | while | flops 1373656064 | bytes 101851632 | solution.py:154
  408.9 4.0 copy-done
  416.3 8.9 %multiply_add_fusion.14 = f32[4,4,5,128,128]{4,3,2,1,0:T(8,128)} fusion(f32[4,4,5,128,128]{4,3,2,1,0:T(8,128)} %get-tuple-element.609, f32[4,4,5,128]{3,2,1,0:T(8,128)S(1)} %get-tuple-element.550, f32[4,4,256,128,5]{3,2,4,1,0:T(8,128)} %copy-done, f32[4,4,5,128]{3,2,1,0:T(8,128)S(1)} %max.41, pred[4,256]{1,0:T(4,128)(4,1)S(1)} %broadcast_bitcast_fusion.2, ...), kind=kOutput, calls=%fused_computation.121.clone.1 | convolution fusion | flops 684195840 | bytes 22103040 | tf_op jit(solution)/shard_map/while/body/tgrqk,tkgd->tgrqd/dot_general | solution.py:42
  434.2 4.0 copy-done
  441.6 8.9 %multiply_add_fusion.14 = f32[4,4,5,128,128]{4,3,2,1,0:T(8,128)} fusion(f32[4,4,5,128,128]{4,3,2,1,0:T(8,128)} %get-tuple-element.609, f32[4,4,5,128]{3,2,1,0:T(8,128)S(1)} %get-tuple-element.550, f32[4,4,256,128,5]{3,2,4,1,0:T(8,128)} %copy-done, f32[4,4,5,128]{3,2,1,0:T(8,128)S(1)} %max.41, pred[4,256]{1,0:T(4,128)(4,1)S(1)} %broadcast_bitcast_fusion.2, ...), kind=kOutput, calls=%fused_computation.121.clone.1 | convolution fusion | flops 684195840 | bytes 22103040 | tf_op jit(solution)/shard_map/while/body/tgrqk,tkgd->tgrqd/dot_general | solution.py:42
  453.9 3.8 copy.195
  457.7 7.0 %reshape.278 = bf16[512,2560]{1,0:T(8,128)(2,1)} reshape(bf16[4,128,4,5,128]{4,3,2,1,0:T(8,128)(2,1)} %copy.195) | data formatting | bytes 5242880 | tf_op jit(solution)/shard_map/convert_element_type | solution.py:158
  (141 shorter events, 82.9 us)
Async XLA Ops:
  6.5 127.4 %all-gather.2.cloned.1.call-start = ((), (), s32[]{:S(2)}) async-start(), calls=%async_computation.2 | async-start | bytes 5242880 | tf_op jit(solution)/shard_map/all_gather | solution.py:76
  9.7 119.8 %copy-start.14 = (bf16[512,2,512]{0,2,1:T(8,128)(2,1)}, bf16[512,2,512]{0,2,1:T(8,128)(2,1)S(1)}, u32[]{:S(2)}) copy-start(bf16[512,2,512]{0,2,1:T(8,128)(2,1)S(1)} %copy.136) | copy-start | bytes 3145732
  9.7 23.6 %collective-permute-start = (bf16[512,2,512]{0,2,1:T(8,128)(2,1)S(1)}, bf16[512,2,512]{0,2,1:T(8,128)(2,1)S(1)}, u32[]{:S(2)}, u32[]{:S(2)}) collective-permute-start(bf16[512,2,512]{0,2,1:T(8,128)(2,1)S(1)} %copy.136), channel_id=1, source_target_pairs={{0,1},{1,2},{2,3},{3,4},{4,5},{5,6},{6,7},{7,8},{8,9},{9,10},{10,1... | collective-permute-start | bytes 3145736 | tf_op jit(solution)/shard_map/ppermute | solution.py:13
  33.3 38.5 %copy-start.16 = (bf16[512,2,512]{0,2,1:T(8,128)(2,1)}, bf16[512,2,512]{0,2,1:T(8,128)(2,1)S(1)}, u32[]{:S(2)}) copy-start(bf16[512,2,512]{0,2,1:T(8,128)(2,1)S(1)} %collective-permute-done) | copy-start | bytes 3145732
  33.3 38.5 %collective-permute-start.1 = (bf16[512,2,512]{0,2,1:T(8,128)(2,1)S(1)}, bf16[512,2,512]{0,2,1:T(8,128)(2,1)S(1)}, u32[]{:S(2)}, u32[]{:S(2)}) collective-permute-start(bf16[512,2,512]{0,2,1:T(8,128)(2,1)S(1)} %collective-permute-done), channel_id=1, source_target_pairs={{0,1},{1,2},{2,3},{3,4},{4,5},{5,6},{6,7},{7,8},{8,9},{9,10},{10,1... | collective-permute-start | bytes 3145736 | tf_op jit(solution)/shard_map/ppermute | solution.py:13
  71.8 57.7 %copy-start.15 = (bf16[512,2,512]{0,2,1:T(8,128)(2,1)}, bf16[512,2,512]{0,2,1:T(8,128)(2,1)S(1)}, u32[]{:S(2)}) copy-start(bf16[512,2,512]{0,2,1:T(8,128)(2,1)S(1)} %collective-permute-done.1) | copy-start | bytes 3145732
  71.8 38.6 %collective-permute-start.2 = (bf16[512,2,512]{0,2,1:T(8,128)(2,1)S(1)}, bf16[512,2,512]{0,2,1:T(8,128)(2,1)}, u32[]{:S(2)}, u32[]{:S(2)}) collective-permute-start(bf16[512,2,512]{0,2,1:T(8,128)(2,1)S(1)} %collective-permute-done.1), channel_id=1, source_target_pairs={{0,1},{1,2},{2,3},{3,4},{4,5},{5,6},{6,7},{7,8},{8,9},{9,10},{10,1... | collective-permute-start | bytes 3145736 | tf_op jit(solution)/shard_map/ppermute | solution.py:13
  110.3 23.0 %collective-permute-start.3 = (bf16[512,2,512]{0,2,1:T(8,128)(2,1)}, bf16[512,2,512]{0,2,1:T(8,128)(2,1)}, u32[]{:S(2)}, u32[]{:S(2)}) collective-permute-start(bf16[512,2,512]{0,2,1:T(8,128)(2,1)} %collective-permute-done.2), channel_id=1, source_target_pairs={{0,1},{1,2},{2,3},{3,4},{4,5},{5,6},{6,7},{7,8},{8,9},{9,10},{10,1... | collective-permute-start | bytes 3145736 | tf_op jit(solution)/shard_map/ppermute | solution.py:13
  111.4 21.8 %all-to-all-start = ((s32[8,1,2]{2,1,0:T(1,128)}), s32[8,1,2]{2,1,0:T(1,128)S(1)}, u32[]{:S(2)}, u32[]{:S(2)}) async-start(s32[8,1,2]{2,1,0:T(1,128)} %bitcast.78), calls=%async_computation | async-start | bytes 8192 | tf_op jit(solution)/shard_map/all_to_all | solution.py:81
  133.3 27.4 %collective-permute-start.4 = (bf16[512,2,512]{0,2,1:T(8,128)(2,1)}, bf16[512,2,512]{0,2,1:T(8,128)(2,1)}, u32[]{:S(2)}, u32[]{:S(2)}) collective-permute-start(bf16[512,2,512]{0,2,1:T(8,128)(2,1)} %collective-permute-done.3), channel_id=1, source_target_pairs={{0,1},{1,2},{2,3},{3,4},{4,5},{5,6},{6,7},{7,8},{8,9},{9,10},{10,1... | collective-permute-start | bytes 3145736 | tf_op jit(solution)/shard_map/ppermute | solution.py:13
  138.9 260.9 %all-to-all-start.1 = ((bf16[8,2,2,128,512]{4,3,2,1,0:T(8,128)(2,1)}), bf16[8,2,2,128,512]{4,3,2,1,0:T(8,128)(2,1)}, u32[]{:S(2)}, u32[]{:S(2)}) async-start(bf16[8,2,2,128,512]{4,3,2,1,0:T(8,128)(2,1)} %bitcast.315), calls=%async_computation.1 | async-start | bytes 8388608 | tf_op jit(solution)/shard_map/all_to_all | solution.py:83
  145.4 9.8 %copy-start.18 = (s32[4]{0:T(128)S(1)}, s32[4]{0:T(128)}, u32[]{:S(2)}) copy-start(s32[4]{0:T(128)} %param.27) | copy-start | bytes 52
  160.7 16.5 %collective-permute-start.5 = (bf16[512,2,512]{0,2,1:T(8,128)(2,1)}, bf16[512,2,512]{0,2,1:T(8,128)(2,1)}, u32[]{:S(2)}, u32[]{:S(2)}) collective-permute-start(bf16[512,2,512]{0,2,1:T(8,128)(2,1)} %collective-permute-done.4), channel_id=1, source_target_pairs={{0,1},{1,2},{2,3},{3,4},{4,5},{5,6},{6,7},{7,8},{8,9},{9,10},{10,1... | collective-permute-start | bytes 3145736 | tf_op jit(solution)/shard_map/ppermute | solution.py:13
  177.2 196.2 %collective-permute-start.6 = (bf16[512,2,512]{0,2,1:T(8,128)(2,1)}, bf16[512,2,512]{0,2,1:T(8,128)(2,1)}, u32[]{:S(2)}, u32[]{:S(2)}) collective-permute-start(bf16[512,2,512]{0,2,1:T(8,128)(2,1)} %collective-permute-done.5), channel_id=1, source_target_pairs={{0,1},{1,2},{2,3},{3,4},{4,5},{5,6},{6,7},{7,8},{8,9},{9,10},{10,1... | collective-permute-start | bytes 3145736 | tf_op jit(solution)/shard_map/ppermute | solution.py:13
  219.9 7.3 %copy-start.1 = (f32[4,512,4,128,5]{3,1,4,2,0:T(8,128)}, f32[4,512,4,128,5]{3,1,4,2,0:T(8,128)S(1)}, u32[]{:S(2)}) copy-start(f32[4,512,4,128,5]{3,1,4,2,0:T(8,128)S(1)} %get-tuple-element.465) | copy-start | bytes 62914564 | tf_op jit(solution)/shard_map/cond
  219.9 7.3 %copy-start.8 = (bf16[512,2,4,128]{3,0,2,1:T(8,128)(2,1)S(1)}, bf16[512,2,4,128]{3,0,2,1:T(8,128)(2,1)}, u32[]{:S(2)}) copy-start(bf16[512,2,4,128]{3,0,2,1:T(8,128)(2,1)} %copy.143) | copy-start | bytes 3145732 | tf_op jit(solution)/shard_map/cond
  246.8 7.3 %copy-start.2 = (f32[4,512,4,128,5]{3,1,4,2,0:T(8,128)}, f32[4,512,4,128,5]{3,1,4,2,0:T(8,128)S(1)}, u32[]{:S(2)}) copy-start(f32[4,512,4,128,5]{3,1,4,2,0:T(8,128)S(1)} %get-tuple-element.467) | copy-start | bytes 62914564 | tf_op jit(solution)/shard_map/cond
  246.8 7.3 %copy-start.9 = (bf16[512,2,4,128]{3,0,2,1:T(8,128)(2,1)S(1)}, bf16[512,2,4,128]{3,0,2,1:T(8,128)(2,1)}, u32[]{:S(2)}) copy-start(bf16[512,2,4,128]{3,0,2,1:T(8,128)(2,1)} %copy.145) | copy-start | bytes 3145732 | tf_op jit(solution)/shard_map/cond
  273.4 7.3 %copy-start.3 = (f32[4,512,4,128,5]{3,1,4,2,0:T(8,128)}, f32[4,512,4,128,5]{3,1,4,2,0:T(8,128)S(1)}, u32[]{:S(2)}) copy-start(f32[4,512,4,128,5]{3,1,4,2,0:T(8,128)S(1)} %get-tuple-element.469) | copy-start | bytes 62914564 | tf_op jit(solution)/shard_map/cond
  273.4 7.3 %copy-start.10 = (bf16[512,2,4,128]{3,0,2,1:T(8,128)(2,1)S(1)}, bf16[512,2,4,128]{3,0,2,1:T(8,128)(2,1)}, u32[]{:S(2)}) copy-start(bf16[512,2,4,128]{3,0,2,1:T(8,128)(2,1)} %copy.147) | copy-start | bytes 3145732 | tf_op jit(solution)/shard_map/cond
  299.9 7.3 %copy-start.4 = (f32[4,512,4,128,5]{3,1,4,2,0:T(8,128)}, f32[4,512,4,128,5]{3,1,4,2,0:T(8,128)S(1)}, u32[]{:S(2)}) copy-start(f32[4,512,4,128,5]{3,1,4,2,0:T(8,128)S(1)} %get-tuple-element.471) | copy-start | bytes 62914564 | tf_op jit(solution)/shard_map/cond
  300.0 7.3 %copy-start.11 = (bf16[512,2,4,128]{3,0,2,1:T(8,128)(2,1)S(1)}, bf16[512,2,4,128]{3,0,2,1:T(8,128)(2,1)}, u32[]{:S(2)}) copy-start(bf16[512,2,4,128]{3,0,2,1:T(8,128)(2,1)} %copy.149) | copy-start | bytes 3145732 | tf_op jit(solution)/shard_map/cond
  326.6 7.3 %copy-start.5 = (f32[4,512,4,128,5]{3,1,4,2,0:T(8,128)}, f32[4,512,4,128,5]{3,1,4,2,0:T(8,128)S(1)}, u32[]{:S(2)}) copy-start(f32[4,512,4,128,5]{3,1,4,2,0:T(8,128)S(1)} %get-tuple-element.473) | copy-start | bytes 62914564 | tf_op jit(solution)/shard_map/cond
  326.6 7.3 %copy-start.12 = (bf16[512,2,4,128]{3,0,2,1:T(8,128)(2,1)S(1)}, bf16[512,2,4,128]{3,0,2,1:T(8,128)(2,1)}, u32[]{:S(2)}) copy-start(bf16[512,2,4,128]{3,0,2,1:T(8,128)(2,1)} %copy.151) | copy-start | bytes 3145732 | tf_op jit(solution)/shard_map/cond
  353.2 7.3 %copy-start.6 = (f32[4,512,4,128,5]{3,1,4,2,0:T(8,128)}, f32[4,512,4,128,5]{3,1,4,2,0:T(8,128)S(1)}, u32[]{:S(2)}) copy-start(f32[4,512,4,128,5]{3,1,4,2,0:T(8,128)S(1)} %get-tuple-element.475) | copy-start | bytes 62914564 | tf_op jit(solution)/shard_map/cond
  353.3 7.3 %copy-start.13 = (bf16[512,2,4,128]{3,0,2,1:T(8,128)(2,1)S(1)}, bf16[512,2,4,128]{3,0,2,1:T(8,128)(2,1)}, u32[]{:S(2)}) copy-start(bf16[512,2,4,128]{3,0,2,1:T(8,128)(2,1)} %copy.153) | copy-start | bytes 3145732 | tf_op jit(solution)/shard_map/cond
  373.4 26.4 %copy-start.17 = (s32[4,2,2]{0,2,1:T(2,128)S(1)}, s32[4,2,2]{0,2,1:T(2,128)}, u32[]{:S(2)}) copy-start(s32[4,2,2]{0,2,1:T(2,128)} %copy.160) | copy-start | bytes 196
  373.4 26.4 %copy-start.19 = (s32[4]{0:T(128)S(1)}, s32[4]{0:T(128)}, u32[]{:S(2)}) copy-start(s32[4]{0:T(128)} %param.27) | copy-start | bytes 52
  378.1 7.0 %copy-start.7 = (f32[4,512,4,128,5]{3,1,4,2,0:T(8,128)}, f32[4,512,4,128,5]{3,1,4,2,0:T(8,128)S(1)}, u32[]{:S(2)}) copy-start(f32[4,512,4,128,5]{3,1,4,2,0:T(8,128)S(1)} %get-tuple-element.477) | copy-start | bytes 62914564 | tf_op jit(solution)/shard_map/cond
  408.9 4.0 copy-start
  434.2 4.0 copy-start
Sparse Core Ops, SparseCore 0:
  8.9 79.2 all-gather.1
where the time goes:
time: 480 us; the launch traced here: 472 us
  matrix products  161 us (34%)
  waiting for transfers between devices  103 us (21%)
  local copies, waits for them, and re-layouts  93.8 us (20%)
  starting transfers between devices  47.9 us (10%)
  other arithmetic  47.7 us (10%)
  between operations  14.4 us (3%)
    dot_general x9, matrix products, absorb(): jnp.einsum(value_form, block_weights.astype(jnp.bfloat16), value_rows, pr...  106 us
    ppermute x7, waiting for transfers between devices, from_behind(): return lax.ppermute(value, axis, pairs)  102 us
    dot_general x9, matrix products, absorb(): jnp.einsum(score_form, queries, key_rows, preferred_element_type=jnp.floa...  33.9 us
    reduce_sum x9, other arithmetic, absorb(): new_sum = old_sum * rescale + jnp.sum(block_weights, axis=-1)  31.4 us
    ppermute x7, starting transfers between devices, from_behind(): return lax.ppermute(value, axis, pairs)  27.7 us
    cond x32, local copies, waits for them, and re-layouts  25.3 us
    all_to_all x1, starting transfers between devices, local(): lax.all_to_all(requests, 'ctx', split_axis=0, concat_axis=0, tiled=True)  13.7 us
    another operation x6, local copies, waits for them, and re-layouts  13.6 us
  transfers between devices with their start and end apart: 10, of which 4 were waited for; matrix products, arithmetic and copies ran while one was open for 45% of the time, Pallas kernels for 0%

commit v1 on v0

v1 whole, which is shorter than its diff:
```python
import functools
import math

import jax
import jax.numpy as jnp
from jax import lax
from jax.experimental import pallas as pl
from jax.experimental.pallas import tpu as pltpu
from jax.sharding import PartitionSpec as P

HEAD = 128
REQ_TILES = 32
CHUNK = 4
SCALE = math.log2(math.e) * HEAD**-0.5


def from_behind(value, axis, steps):
    count = lax.axis_size(axis)
    pairs = [(source, (source + steps) % count) for source in range(count)]
    return lax.ppermute(value, axis, pairs)


def request_table(dest_index, live_mask, count_dest, capacity, payload):
    onehot = (
        (dest_index[:, None] == jnp.arange(count_dest, dtype=jnp.int32)[None, :])
        & live_mask[:, None]
    ).astype(jnp.int32)
    rank_within = jnp.sum(onehot * (jnp.cumsum(onehot, axis=0) - 1), axis=1)
    position = dest_index * capacity + rank_within
    target = jnp.where(live_mask, position, -1)
    slot_ids = jnp.arange(count_dest * capacity, dtype=jnp.int32)
    requests = jnp.max(
        jnp.where(target[:, None] == slot_ids[None, :], payload[:, None], -1), axis=0
    )
    return (requests.reshape(count_dest, capacity), position)


def absorb(index, key_rows, value_rows, mask, first, qs, top, acc):
    scores = lax.dot_general(
        qs[index], key_rows, (((1,), (1,)), ((), ())), preferred_element_type=jnp.float32
    )
    if mask is not None:
        scores = jnp.where(mask, scores, -jnp.inf)
    block_max = jnp.max(scores, axis=1, keepdims=True)
    ones = jnp.ones_like(value_rows)
    values = jnp.concatenate([value_rows, ones], axis=1)
    if first:
        new_max = jnp.broadcast_to(block_max, top.shape[1:])
        weights = jnp.exp2((scores - block_max) * SCALE).astype(jnp.bfloat16)
        acc[index] = jnp.dot(weights, values, preferred_element_type=jnp.float32)
    else:
        old_max = top[index]
        new_max = jnp.maximum(old_max, block_max)
        wide = jnp.concatenate([new_max] * (scores.shape[1] // HEAD), axis=1)
        weights = jnp.exp2((scores - wide) * SCALE).astype(jnp.bfloat16)
        rescale = jnp.exp2((old_max - new_max) * SCALE)
        acc[index] = acc[index] * jnp.concatenate([rescale, rescale], axis=1) + jnp.dot(
            weights, values, preferred_element_type=jnp.float32
        )
    top[index] = new_max


def head_lanes(group):
    return pl.ds(pl.multiple_of(group * HEAD, HEAD), HEAD)


def own_block(own, tile_num, groups, qs, top, acc):
    tile_rows = own.shape[0] // tile_num
    repeat = qs.shape[1] // tile_rows
    shape = (repeat * tile_rows, own.shape[0])
    query_row = lax.rem(lax.broadcasted_iota(jnp.int32, shape, 0), tile_rows)
    key_row = lax.broadcasted_iota(jnp.int32, shape, 1)

    def body(index, carry):
        group, tile = lax.div(index, tile_num), lax.rem(index, tile_num)
        lanes = head_lanes(group)
        keys = own[:, lanes]
        values = own[:, pl.ds(pl.multiple_of((groups + group) * HEAD, HEAD), HEAD)]
        mask = key_row <= query_row + tile * tile_rows
        absorb(index, keys, values, mask, True, qs, top, acc)
        return carry

    lax.fori_loop(0, groups * tile_num, body, 0)


def earlier_block(block, tile_num, groups, qs, top, acc):
    def body(group, carry):
        keys = block[:, head_lanes(group)]
        values = block[:, pl.ds(pl.multiple_of((groups + group) * HEAD, HEAD), HEAD)]
        for tile in range(tile_num):
            absorb(group * tile_num + tile, keys, values, None, False, qs, top, acc)
        return carry

    lax.fori_loop(0, groups, body, 0)


def branch_blocks(position, count, received, tile_num, list_len, groups, qs, top, acc):
    block_len = received.shape[2]
    shape = (qs.shape[1], CHUNK * block_len)
    key_block = lax.div(lax.broadcasted_iota(jnp.int32, shape, 1), block_len)

    def body(index, carry):
        group, tile = lax.div(index, tile_num), lax.rem(index, tile_num)
        lanes = head_lanes(group)
        for start in range(0, list_len, CHUNK):
            where = [position[tile * list_len + start + i] for i in range(CHUNK)]
            keys = jnp.concatenate([received[w, 0, :, lanes] for w in where], axis=0)
            values = jnp.concatenate([received[w, 1, :, lanes] for w in where], axis=0)
            mask = key_block < count[tile] - start
            absorb(index, keys, values, mask, False, qs, top, acc)
        return carry

    lax.fori_loop(0, groups * tile_num, body, 0)


def load_queries(q_ref, tile_num, groups, qs):
    tile_rows = q_ref.shape[0] // tile_num
    repeat = qs.shape[1] // tile_rows
    for group in range(groups):
        for tile in range(tile_num):
            for r in range(repeat):
                head = group * repeat + r
                qs[group * tile_num + tile, r * tile_rows : (r + 1) * tile_rows, :] = q_ref[
                    tile * tile_rows : (tile + 1) * tile_rows, head * HEAD : (head + 1) * HEAD
                ]


def store_result(o_ref, tile_num, groups, acc):
    tile_rows = o_ref.shape[0] // tile_num
    repeat = acc.shape[1] // tile_rows
    for group in range(groups):
        for tile in range(tile_num):
            for r in range(repeat):
                head = group * repeat + r
                part = acc[group * tile_num + tile, r * tile_rows : (r + 1) * tile_rows, :]
                o_ref[
                    tile * tile_rows : (tile + 1) * tile_rows, head * HEAD : (head + 1) * HEAD
                ] = (part[:, :HEAD] / part[:, HEAD:]).astype(o_ref.dtype)


def attend(tile_num, list_len, groups, position, count, place, q_ref, own, earlier, received, o_ref, qs, top, acc):
    load_queries(q_ref, tile_num, groups, qs)
    own_block(own, tile_num, groups, qs, top, acc)

    def body(step, carry):
        earlier_block(earlier.at[step], tile_num, groups, qs, top, acc)
        return carry

    lax.fori_loop(0, place[0], body, 0)
    branch_blocks(position, count, received, tile_num, list_len, groups, qs, top, acc)
    store_result(o_ref, tile_num, groups, acc)


def local(summary_q, summary_kv, kv_cache, block_slot, tile_blocks, tile_count):
    shards = lax.axis_size("ctx")
    tile_num, list_len = tile_blocks.shape
    blk_dev = kv_cache.shape[0]
    block_len = kv_cache.shape[2]
    kv_width = kv_cache.shape[3]
    groups = kv_width // HEAD
    rows = summary_q.shape[0]
    tile_rows = rows // tile_num
    repeat = summary_q.shape[1] // kv_width
    col_cap = max(2, -(-(tile_num * list_len) // shards))
    req_devs = REQ_TILES // tile_num
    entries = tile_blocks.reshape(-1)
    live_mask = (jnp.arange(list_len, dtype=jnp.int32)[None, :] < tile_count[:, None]).reshape(-1)
    block_ids = jnp.arange(block_slot.shape[0], dtype=jnp.int32)
    stored_at = jnp.sum(
        jnp.where(entries[:, None] == block_ids[None, :], block_slot[None, :], 0), axis=1
    )
    owner_dev = stored_at // blk_dev
    local_slot = stored_at % blk_dev
    column = lax.all_gather(kv_cache, "branch", axis=0, tiled=True)
    requests, position = request_table(
        owner_dev % shards, live_mask, shards, col_cap, owner_dev // shards * blk_dev + local_slot
    )
    payload = column[
        jnp.maximum(lax.all_to_all(requests, "ctx", split_axis=0, concat_axis=0, tiled=True), 0)
    ]
    received = lax.all_to_all(payload, "ctx", split_axis=0, concat_axis=0, tiled=True)
    received = received.reshape(-1, 2, block_len, kv_width)
    position = jnp.where(live_mask, position, 0)
    flat_index = lax.axis_index("branch") * shards + lax.axis_index("ctx")
    place = (flat_index - 1 + req_devs) % req_devs
    own = summary_kv.reshape(rows, 2 * kv_width)
    passed = own
    earlier = []
    for _ in range(1, req_devs):
        passed = from_behind(passed, ("branch", "ctx"), 1)
        earlier.append(passed)
    vmem, smem = pl.BlockSpec(memory_space=pltpu.VMEM), pl.BlockSpec(memory_space=pltpu.SMEM)
    return pl.pallas_call(
        functools.partial(attend, tile_num, list_len, groups),
        out_shape=jax.ShapeDtypeStruct(summary_q.shape, jnp.bfloat16),
        in_specs=[smem] * 3 + [vmem] * 4,
        out_specs=vmem,
        scratch_shapes=[
            pltpu.VMEM((groups * tile_num, repeat * tile_rows, HEAD), jnp.bfloat16),
            pltpu.VMEM((groups * tile_num, repeat * tile_rows, HEAD), jnp.float32),
            pltpu.VMEM((groups * tile_num, repeat * tile_rows, 2 * HEAD), jnp.float32),
        ],
        compiler_params=pltpu.CompilerParams(vmem_limit_bytes=60 * 2**20),
    )(position, tile_count, place[None], summary_q, own, jnp.stack(earlier), received)


def solution(mesh):
    in_specs = (
        P(("branch", "ctx"), None),
        P(("branch", "ctx"), None, None),
        P(("branch", "ctx"), None, None, None),
        P(),
        P(("branch", "ctx"), None),
        P(("branch", "ctx")),
    )
    out_specs = P(("branch", "ctx"), None)
    return jax.shard_map(local, mesh=mesh, in_specs=in_specs, out_specs=out_specs, check_vma=False)
```

time: 480 us -> 320 us (0.67); the launches traced: 472 us -> 317 us
  matrix products: 161 us -> 0 us
  Pallas kernels: 0 us -> 92.3 us
  local copies, waits for them, and re-layouts: 93.8 us -> 18.7 us
  other arithmetic: 47.7 us -> 2.5 us
  blocking collectives: 0 us -> 16.6 us
  waiting for transfers between devices: 103 us -> 117 us
  starting transfers between devices: 47.9 us -> 56.7 us
    dot_general x20 -> x0, matrix products: 161 us -> none  [the longest x9 106 us: absorb(): jnp.einsum(value_form, block_weights.astype(jnp.bfloat16), value_rows, pr...]
    pallas_call x0 -> x1, Pallas kernels: none -> 92.3 us  [local(): pl.pallas_call(functools.partial(attend, tile_num, list_len, groups), out...]
    reduce_sum x10 -> x0, other arithmetic: 40.9 us -> none  [the longest x9 31.4 us: absorb(): new_sum = old_sum * rescale + jnp.sum(block_weights, axis=-1)]
    cond x32 -> x0, local copies, waits for them, and re-layouts: 25.3 us -> none
    ppermute x7, starting transfers between devices: 27.7 us -> 52.2 us  [from_behind(): return lax.ppermute(value, axis, pairs)]
    while x13 -> x0, local copies, waits for them, and re-layouts: 17.3 us -> none
    all_to_all x0 -> x1, blocking collectives: none -> 16.6 us  [local(): lax.all_to_all(requests, 'ctx', split_axis=0, concat_axis=0, tiled=True)]
    all_to_all x1 -> x0, starting transfers between devices: 13.7 us -> none  [local(): lax.all_to_all(requests, 'ctx', split_axis=0, concat_axis=0, tiled=True)]
  transfers between devices with their start and end apart: 10 -> 9, of which waited for: 4 -> 5; matrix products, arithmetic and copies ran while one was open for 45% -> 7% of each run, Pallas kernels for 0% -> 0%
where the time goes in v1:
time: 320 us; the launch traced here: 317 us
  waiting for transfers between devices  117 us (37%)
  Pallas kernels  92.3 us (29%)
  starting transfers between devices  56.7 us (18%)
  local copies, waits for them, and re-layouts  18.7 us (6%)
  blocking collectives  16.6 us (5%)
  between operations  13.5 us (4%)
    ppermute x7, waiting for transfers between devices, from_behind(): return lax.ppermute(value, axis, pairs)  112 us
    pallas_call x1, Pallas kernels, local(): pl.pallas_call(functools.partial(attend, tile_num, list_len, groups), out...  92.3 us
    ppermute x7, starting transfers between devices, from_behind(): return lax.ppermute(value, axis, pairs)  52.2 us
    all_to_all x1, blocking collectives, local(): lax.all_to_all(requests, 'ctx', split_axis=0, concat_axis=0, tiled=True)  16.6 us
    unnamed x9, local copies, waits for them, and re-layouts  11.5 us
  transfers between devices with their start and end apart: 9, of which 5 were waited for; matrix products, arithmetic and copies ran while one was open for 7% of the time, Pallas kernels for 0%

profile of v1, /device:TPU:8, one launch (start us, length us, event | category | flops | bytes accessed | tf_op | source)
XLA Modules:
  0.0 316.9 jit_solution(13412340489708496255)
XLA Ops:
  6.5 0.0 all-gather.2.cloned.1.call-start
  6.5 0.7 all-gather.2.cloned.1.call-update
  7.3 1.5 copy.9
  8.7 0.0 copy-start
  8.7 0.1 collective-permute-start
  8.8 21.5 %collective-permute-done = bf16[512,1024]{1,0:T(8,128)(2,1)S(1)} collective-permute-done((bf16[512,1024]{1,0:T(8,128)(2,1)S(1)}, bf16[512,1024]{1,0:T(8,128)(2,1)S(1)}, u32[]{:S(2)}, u32[]{:S(2)}) %collective-permute-start) | collective-permute-done | bytes 1048608 | tf_op jit(solution)/shard_map/ppermute | solution.py:20
  30.4 0.0 collective-permute-start.1
  30.4 38.6 %collective-permute-done.1 = bf16[512,1024]{1,0:T(8,128)(2,1)} collective-permute-done((bf16[512,1024]{1,0:T(8,128)(2,1)S(1)}, bf16[512,1024]{1,0:T(8,128)(2,1)}, u32[]{:S(2)}, u32[]{:S(2)}) %collective-permute-start.1) | collective-permute-done | bytes 1048608 | tf_op jit(solution)/shard_map/ppermute | solution.py:20
  68.9 0.0 collective-permute-start.2
  68.9 0.7 iota_compare_fusion.3
  69.7 0.1 lt.44
  69.7 0.8 eq.46
  70.5 0.8 select_reduce_fusion.2
  71.4 36.2 %collective-permute-done.2 = bf16[512,1024]{1,0:T(8,128)(2,1)S(1)} collective-permute-done((bf16[512,1024]{1,0:T(8,128)(2,1)}, bf16[512,1024]{1,0:T(8,128)(2,1)S(1)}, u32[]{:S(2)}, u32[]{:S(2)}) %collective-permute-start.2) | collective-permute-done | bytes 1048608 | tf_op jit(solution)/shard_map/ppermute | solution.py:20
  107.6 0.0 collective-permute-start.3
  107.6 0.1 fusion.1
  107.7 0.2 select_reduce_fusion.1
  107.9 0.5 broadcast_select_fusion
  108.4 0.1 select_reduce_fusion
  108.5 0.1 all_to_all.9
  108.6 16.6 %all_to_all.14 = s32[8,1,2]{2,1,0:T(1,128)S(1)} all-to-all(s32[8,1,2]{2,1,0:T(1,128)S(1)} %bitcast.24), channel_id=1, replica_groups=mesh['branch'=4,'ctx'=8] {'ctx'}, dimensions={0} | all-to-all | bytes 128 | tf_op jit(solution)/shard_map/all_to_all | solution.py:179
  125.2 0.1 reshape.117
  125.3 0.0 all-gather.2.cloned.1.call-done
  125.3 5.0 %gather_fusion = bf16[16,2,128,512]{3,2,1,0:T(8,128)(2,1)} fusion(bf16[16,2,128,512]{3,2,1,0:T(8,128)(2,1)} %all-gather.2.cloned.1.call-done, s32[1024]{0:T(1024)S(1)} %pad_clamp_fusion), kind=kCustom, calls=%fused_computation | custom fusion | bytes 8388672 | tf_op jit(solution)/shard_map/gather | solution.py:178
  130.4 0.0 copy-done
  130.4 4.5 %all-to-all-start.1 = ((bf16[8,2,2,128,512]{4,3,2,1,0:T(8,128)(2,1)}), bf16[8,2,2,128,512]{4,3,2,1,0:T(8,128)(2,1)}, u32[]{:S(2)}, u32[]{:S(2)}) async-start(bf16[8,2,2,128,512]{4,3,2,1,0:T(8,128)(2,1)} %bitcast.20), calls=%async_computation.1 | async-start | bytes 8388608 | tf_op jit(solution)/shard_map/all_to_all | solution.py:181
  134.9 0.0 collective-permute-done.3
  134.9 0.4 collective-permute-start.4
  135.3 16.1 %collective-permute-done.4 = bf16[512,1024]{1,0:T(8,128)(2,1)S(1)} collective-permute-done((bf16[512,1024]{1,0:T(8,128)(2,1)}, bf16[512,1024]{1,0:T(8,128)(2,1)S(1)}, u32[]{:S(2)}, u32[]{:S(2)}) %collective-permute-start.4) | collective-permute-done | bytes 1048608 | tf_op jit(solution)/shard_map/ppermute | solution.py:20
  151.4 41.0 %collective-permute-start.5 = (bf16[512,1024]{1,0:T(8,128)(2,1)S(1)}, bf16[512,1024]{1,0:T(8,128)(2,1)}, u32[]{:S(2)}, u32[]{:S(2)}) collective-permute-start(bf16[512,1024]{1,0:T(8,128)(2,1)S(1)} %collective-permute-done.4), channel_id=1, source_target_pairs={{0,1},{1,2},{2,3},{3,4},{4,5},{5,6},{6,7},{7,8},{8,9},{9,10},{10,1... | collective-permute-start | bytes 3145736 | tf_op jit(solution)/shard_map/ppermute | solution.py:20
  192.4 1.1 bitcast_dynamic-update-slice_fusion.6
  193.4 2.3 bitcast_dynamic-update-slice_fusion.5
  195.8 0.0 collective-permute-done.5
  195.8 10.7 %collective-permute-start.6 = (bf16[512,1024]{1,0:T(8,128)(2,1)}, bf16[512,1024]{1,0:T(8,128)(2,1)S(1)}, u32[]{:S(2)}, u32[]{:S(2)}) collective-permute-start(bf16[512,1024]{1,0:T(8,128)(2,1)} %collective-permute-done.5), channel_id=1, source_target_pairs={{0,1},{1,2},{2,3},{3,4},{4,5},{5,6},{6,7},{7,8},{8,9},{9,10},{10,1... | collective-permute-start | bytes 3145736 | tf_op jit(solution)/shard_map/ppermute | solution.py:20
  206.5 1.1 bitcast_dynamic-update-slice_fusion.4
  207.6 2.3 bitcast_dynamic-update-slice_fusion.3
  209.8 1.0 bitcast_dynamic-update-slice_fusion.2
  210.9 2.3 bitcast_dynamic-update-slice_fusion.1
  213.2 0.0 collective-permute-done.6
  213.2 1.1 bitcast_dynamic-update-slice_fusion.earlier
  214.3 3.5 %all-to-all-done.1 = bf16[8,2,2,128,512]{4,3,2,1,0:T(8,128)(2,1)} async-done(((bf16[8,2,2,128,512]{4,3,2,1,0:T(8,128)(2,1)}), bf16[8,2,2,128,512]{4,3,2,1,0:T(8,128)(2,1)}, u32[]{:S(2)}, u32[]{:S(2)}) %all-to-all-start.1) | async-done | bytes 4194336 | tf_op jit(solution)/shard_map/all_to_all | solution.py:181
  217.8 92.3 %shard_map.64 = bf16[512,2560]{1,0:T(8,128)(2,1)} custom-call(s32[16]{0:T(128)} %get-tuple-element.8.position, s32[4]{0:T(128)} %count.1, s32[1]{0:T(128)} %bitcast.place, bf16[512,2560]{1,0:T(8,128)(2,1)} %q_ref.1, bf16[512,1024]{1,0:T(8,128)(2,1)} %bitcast.22, bf16[7,512,1024]{2,1,0:T(8,128)(2,1)} %bitcast_dynamic-update-slice_fusion.earlier, ...), custom_call_target="tpu_custom_call" | custom-call | tf_op jit(solution)/shard_map/pallas_call | solution.py:193
  (5 shorter events, 0.1 us)
Async XLA Ops:
  6.5 118.8 %all-gather.2.cloned.1.call-start = ((), (), s32[]{:S(2)}) async-start(), calls=%async_computation.2 | async-start | bytes 5242880 | tf_op jit(solution)/shard_map/all_gather | solution.py:174
  8.7 121.6 %copy-start = (bf16[64,8,2,512]{3,1,2,0:T(8,128)(2,1)}, bf16[64,8,2,512]{3,1,2,0:T(8,128)(2,1)S(1)}, u32[]{:S(2)}) copy-start(bf16[64,8,2,512]{3,1,2,0:T(8,128)(2,1)S(1)} %copy.9) | copy-start | bytes 3145732
  8.7 21.6 %collective-permute-start = (bf16[512,1024]{1,0:T(8,128)(2,1)S(1)}, bf16[512,1024]{1,0:T(8,128)(2,1)S(1)}, u32[]{:S(2)}, u32[]{:S(2)}) collective-permute-start(bf16[512,1024]{1,0:T(8,128)(2,1)S(1)} %bitcast.21), channel_id=1, source_target_pairs={{0,1},{1,2},{2,3},{3,4},{4,5},{5,6},{6,7},{7,8},{8,9},{9,10},{10,1... | collective-permute-start | bytes 3145736 | tf_op jit(solution)/shard_map/ppermute | solution.py:20
  30.4 38.6 %collective-permute-start.1 = (bf16[512,1024]{1,0:T(8,128)(2,1)S(1)}, bf16[512,1024]{1,0:T(8,128)(2,1)}, u32[]{:S(2)}, u32[]{:S(2)}) collective-permute-start(bf16[512,1024]{1,0:T(8,128)(2,1)S(1)} %collective-permute-done), channel_id=1, source_target_pairs={{0,1},{1,2},{2,3},{3,4},{4,5},{5,6},{6,7},{7,8},{8,9},{9,10},{10,1... | collective-permute-start | bytes 3145736 | tf_op jit(solution)/shard_map/ppermute | solution.py:20
  68.9 38.7 %collective-permute-start.2 = (bf16[512,1024]{1,0:T(8,128)(2,1)}, bf16[512,1024]{1,0:T(8,128)(2,1)S(1)}, u32[]{:S(2)}, u32[]{:S(2)}) collective-permute-start(bf16[512,1024]{1,0:T(8,128)(2,1)} %collective-permute-done.1), channel_id=1, source_target_pairs={{0,1},{1,2},{2,3},{3,4},{4,5},{5,6},{6,7},{7,8},{8,9},{9,10},{10,1... | collective-permute-start | bytes 3145736 | tf_op jit(solution)/shard_map/ppermute | solution.py:20
  107.6 27.3 %collective-permute-start.3 = (bf16[512,1024]{1,0:T(8,128)(2,1)S(1)}, bf16[512,1024]{1,0:T(8,128)(2,1)}, u32[]{:S(2)}, u32[]{:S(2)}) collective-permute-start(bf16[512,1024]{1,0:T(8,128)(2,1)S(1)} %collective-permute-done.2), channel_id=1, source_target_pairs={{0,1},{1,2},{2,3},{3,4},{4,5},{5,6},{6,7},{7,8},{8,9},{9,10},{10,1... | collective-permute-start | bytes 3145736 | tf_op jit(solution)/shard_map/ppermute | solution.py:20
  130.4 87.4 %all-to-all-start.1 = ((bf16[8,2,2,128,512]{4,3,2,1,0:T(8,128)(2,1)}), bf16[8,2,2,128,512]{4,3,2,1,0:T(8,128)(2,1)}, u32[]{:S(2)}, u32[]{:S(2)}) async-start(bf16[8,2,2,128,512]{4,3,2,1,0:T(8,128)(2,1)} %bitcast.20), calls=%async_computation.1 | async-start | bytes 8388608 | tf_op jit(solution)/shard_map/all_to_all | solution.py:181
  134.9 16.4 %collective-permute-start.4 = (bf16[512,1024]{1,0:T(8,128)(2,1)}, bf16[512,1024]{1,0:T(8,128)(2,1)S(1)}, u32[]{:S(2)}, u32[]{:S(2)}) collective-permute-start(bf16[512,1024]{1,0:T(8,128)(2,1)} %collective-permute-done.3), channel_id=1, source_target_pairs={{0,1},{1,2},{2,3},{3,4},{4,5},{5,6},{6,7},{7,8},{8,9},{9,10},{10,1... | collective-permute-start | bytes 3145736 | tf_op jit(solution)/shard_map/ppermute | solution.py:20
  151.4 44.4 %collective-permute-start.5 = (bf16[512,1024]{1,0:T(8,128)(2,1)S(1)}, bf16[512,1024]{1,0:T(8,128)(2,1)}, u32[]{:S(2)}, u32[]{:S(2)}) collective-permute-start(bf16[512,1024]{1,0:T(8,128)(2,1)S(1)} %collective-permute-done.4), channel_id=1, source_target_pairs={{0,1},{1,2},{2,3},{3,4},{4,5},{5,6},{6,7},{7,8},{8,9},{9,10},{10,1... | collective-permute-start | bytes 3145736 | tf_op jit(solution)/shard_map/ppermute | solution.py:20
  195.8 17.4 %collective-permute-start.6 = (bf16[512,1024]{1,0:T(8,128)(2,1)}, bf16[512,1024]{1,0:T(8,128)(2,1)S(1)}, u32[]{:S(2)}, u32[]{:S(2)}) collective-permute-start(bf16[512,1024]{1,0:T(8,128)(2,1)} %collective-permute-done.5), channel_id=1, source_target_pairs={{0,1},{1,2},{2,3},{3,4},{4,5},{5,6},{6,7},{7,8},{8,9},{9,10},{10,1... | collective-permute-start | bytes 3145736 | tf_op jit(solution)/shard_map/ppermute | solution.py:20
Sparse Core Ops, SparseCore 0:
  8.9 79.2 all-gather.1

commit v2 on v1

v2 whole, which is shorter than its diff:
```python
import functools
import math

import jax
import jax.numpy as jnp
from jax import lax
from jax.experimental import pallas as pl
from jax.experimental.pallas import tpu as pltpu
from jax.sharding import PartitionSpec as P

HEAD = 128
REQ_TILES = 32
CHUNK = 4
HALVES = 2
STAGES = 7
SCALE = math.log2(math.e) * HEAD**-0.5


def request_table(dest_index, live_mask, count_dest, capacity, payload):
    onehot = (
        (dest_index[:, None] == jnp.arange(count_dest, dtype=jnp.int32)[None, :])
        & live_mask[:, None]
    ).astype(jnp.int32)
    rank_within = jnp.sum(onehot * (jnp.cumsum(onehot, axis=0) - 1), axis=1)
    position = dest_index * capacity + rank_within
    target = jnp.where(live_mask, position, -1)
    slot_ids = jnp.arange(count_dest * capacity, dtype=jnp.int32)
    requests = jnp.max(
        jnp.where(target[:, None] == slot_ids[None, :], payload[:, None], -1), axis=0
    )
    return (requests.reshape(count_dest, capacity), position)


def absorb(group, tile, key_rows, value_rows, mask, first, q_ref, top, acc):
    groups, tile_num = acc.shape[:2]
    tile_rows = q_ref.shape[0] // tile_num
    repeat = q_ref.shape[1] // (groups * HEAD)
    token = pl.ds(pl.multiple_of(tile * tile_rows, tile_rows), tile_rows)
    index = (group, tile)
    queries = jnp.concatenate(
        [q_ref[token, head_lanes(group * repeat + r)] for r in range(repeat)], axis=0
    )
    scores = lax.dot_general(
        queries, key_rows, (((1,), (1,)), ((), ())), preferred_element_type=jnp.float32
    )
    if mask is not None:
        scores = jnp.where(mask, scores, -jnp.inf)
    block_max = jnp.max(scores, axis=1, keepdims=True)
    ones = jnp.ones_like(value_rows)
    values = jnp.concatenate([value_rows, ones], axis=1)
    if first:
        new_max = jnp.broadcast_to(block_max, top.shape[2:])
        weights = jnp.exp2((scores - block_max) * SCALE).astype(jnp.bfloat16)
        acc[index] = jnp.dot(weights, values, preferred_element_type=jnp.float32)
    else:
        old_max = top[index]
        new_max = jnp.maximum(old_max, block_max)
        wide = jnp.concatenate([new_max] * (scores.shape[1] // HEAD), axis=1)
        weights = jnp.exp2((scores - wide) * SCALE).astype(jnp.bfloat16)
        rescale = jnp.exp2((old_max - new_max) * SCALE)
        acc[index] = acc[index] * jnp.concatenate([rescale, rescale], axis=1) + jnp.dot(
            weights, values, preferred_element_type=jnp.float32
        )
    top[index] = new_max


def head_lanes(group):
    return pl.ds(pl.multiple_of(group * HEAD, HEAD), HEAD)


def own_block(own, q_ref, top, acc):
    groups, tile_num = acc.shape[:2]
    tile_rows = own.shape[0] // tile_num
    shape = (acc.shape[2], own.shape[0])
    query_row = lax.rem(lax.broadcasted_iota(jnp.int32, shape, 0), tile_rows)
    key_row = lax.broadcasted_iota(jnp.int32, shape, 1)

    def body(group, carry):
        keys, values = own[:, head_lanes(group)], own[:, head_lanes(groups + group)]
        for tile in range(tile_num):
            mask = key_row <= query_row + tile * tile_rows
            absorb(group, tile, keys, values, mask, True, q_ref, top, acc)
        return carry

    lax.fori_loop(0, groups, body, 0)


def earlier_block(block, q_ref, top, acc):
    groups, tile_num = acc.shape[:2]

    def body(group, carry):
        keys, values = block[:, head_lanes(group)], block[:, head_lanes(groups + group)]
        for tile in range(tile_num):
            absorb(group, tile, keys, values, None, False, q_ref, top, acc)
        return carry

    lax.fori_loop(0, groups, body, 0)


def branch_blocks(half, position, count, received, q_ref, top, acc):
    groups, tile_num = acc.shape[:2]
    list_len = position.shape[0] // tile_num
    block_len = received.shape[2]
    shape = (acc.shape[2], CHUNK * block_len)
    key_block = lax.div(lax.broadcasted_iota(jnp.int32, shape, 1), block_len)

    def body(tile, carry):
        for start in range(0, list_len, CHUNK):
            where = [position[tile * list_len + start + i] for i in range(CHUNK)]
            mask = key_block < count[tile] - start
            for sub in range(groups // HALVES):
                lanes = slice(sub * HEAD, (sub + 1) * HEAD)
                keys = jnp.concatenate([received[w, 0, :, lanes] for w in where], axis=0)
                values = jnp.concatenate([received[w, 1, :, lanes] for w in where], axis=0)
                group = half * (groups // HALVES) + sub
                absorb(group, tile, keys, values, mask, False, q_ref, top, acc)
        return carry

    lax.fori_loop(0, tile_num, body, 0)


def store_result(o_ref, acc):
    groups, tile_num, stacked, _ = acc.shape
    tile_rows = o_ref.shape[0] // tile_num
    repeat = stacked // tile_rows

    def body(group, carry):
        for tile in range(tile_num):
            for r in range(repeat):
                part = acc[group, tile, r * tile_rows : (r + 1) * tile_rows, :]
                o_ref[
                    tile * tile_rows : (tile + 1) * tile_rows, head_lanes(group * repeat + r)
                ] = (part[:, :HEAD] / part[:, HEAD:]).astype(o_ref.dtype)
        return carry

    lax.fori_loop(0, groups, body, 0)


def join(
    planes, shards, capacity,
    wanted, position, count, q_ref, own, cache, o_ref,
    earlier, relay, column, payload, received, top, acc,
    kv_send, kv_recv, hop_sem, fwd_send, gather_send, gather_recv, list_send, list_recv,
):
    z, c = lax.axis_index("branch"), lax.axis_index("ctx")
    req_devs = earlier.shape[0] + 1
    place = lax.rem(c + req_devs - 1, req_devs)
    crosses = c >= shards - (req_devs - 1)
    blk_dev = cache.shape[0]
    slots = payload.shape[1]
    half_width = cache.shape[3] // HALVES
    slot_len = payload.shape[2]

    def remote(src, dst, send, recv, to):
        return pltpu.make_async_remote_copy(
            src_ref=src, dst_ref=dst, send_sem=send, recv_sem=recv,
            device_id=to, device_id_type=pl.DeviceIdType.MESH,
        )

    def plane_peer(step):
        return (z, lax.rem(c + step, shards))

    def line_peer(step):
        return (lax.rem(z + step, planes), c)

    barrier = pltpu.get_barrier_semaphore()
    for step in range(1, shards):
        pl.semaphore_signal(barrier, inc=1, device_id=plane_peer(step), device_id_type=pl.DeviceIdType.MESH)
    for step in range(1, planes):
        pl.semaphore_signal(barrier, inc=1, device_id=line_peer(step), device_id_type=pl.DeviceIdType.MESH)
    pl.semaphore_wait(barrier, shards + planes - 2)

    hop = remote(own, relay, hop_sem.at[0], hop_sem.at[1], line_peer(1))
    pl.when(crosses)(hop.start)
    pushes = []
    for step in range(1, req_devs):
        push = remote(own, earlier.at[place], kv_send.at[step - 1], kv_recv.at[place], plane_peer(step))
        sends = jnp.logical_and(place + step < req_devs, c + step < shards)
        pl.when(sends)(push.start)
        pushes.append((sends, push))

    gathers = []
    for half in range(HALVES):
        lanes = pl.ds(half * half_width, half_width)
        for step in range(1, planes):
            copy = remote(
                cache.at[:, :, :, lanes], column[half].at[pl.ds(z * blk_dev, blk_dev)],
                gather_send.at[half, step - 1], gather_recv.at[half, step - 1], line_peer(step),
            )
            copy.start()
            gathers.append(copy)
    for half in range(HALVES):
        column[half][pl.ds(z * blk_dev, blk_dev)] = cache[:, :, :, half * half_width : (half + 1) * half_width]

    own_block(own, q_ref, top, acc)

    def absorb_earlier(step, carry):
        slot = jnp.where(c == 0, step, place - 1 - step)
        remote(earlier.at[slot], earlier.at[slot], kv_send.at[0], kv_recv.at[slot], plane_peer(1)).wait_recv()
        earlier_block(earlier.at[slot], q_ref, top, acc)
        return carry

    def send_listed(half):
        for step in range(1, planes):
            gathers[half * (planes - 1) + step - 1].wait_recv()
        copies = []
        for step in range(shards):
            to = lax.rem(c + step, shards)
            slot = 0 if step == 0 else (step - 1) % slots
            if step > slots:
                copies[step - slots - 1].wait_send()
            target = received[half].at[pl.ds(c * capacity, capacity)]
            for i in range(capacity):
                block = column[half][wanted[to * capacity + i]]
                if step == 0:
                    received[half][c * capacity + i] = block
                else:
                    payload[half, slot, i] = block
            if step > 0:
                copy = remote(
                    payload.at[half, slot], target, list_send.at[half, slot],
                    list_recv.at[half, step - 1], plane_peer(step),
                )
                copy.start()
                copies.append(copy)
        return copies

    first = jnp.minimum(place, 1)
    later = jnp.minimum(place, req_devs - 3)
    lax.fori_loop(0, first, absorb_earlier, 0)
    forward = remote(relay, earlier.at[place], fwd_send, kv_recv.at[place], (z, 0))

    @pl.when(crosses)
    def _():
        hop.wait_recv()
        forward.start()

    lax.fori_loop(first, later, absorb_earlier, 0)
    lists = [send_listed(0)]
    lax.fori_loop(later, place, absorb_earlier, 0)
    for half in range(1, HALVES):
        lists.append(send_listed(half))
    for half in range(HALVES):
        for copy in lists[half]:
            copy.wait_recv()
        branch_blocks(half, position, count, received[half], q_ref, top, acc)
    store_result(o_ref, acc)

    pl.when(crosses)(hop.wait_send)
    pl.when(crosses)(forward.wait_send)
    for sends, push in pushes:
        pl.when(sends)(push.wait_send)
    for copy in gathers:
        copy.wait_send()
    for copies in lists:
        for copy in copies[-slots:]:
            copy.wait_send()


def local(summary_q, summary_kv, kv_cache, block_slot, tile_blocks, tile_count):
    planes, shards = lax.axis_size("branch"), lax.axis_size("ctx")
    tile_num, list_len = tile_blocks.shape
    blk_dev = kv_cache.shape[0]
    block_len = kv_cache.shape[2]
    kv_width = kv_cache.shape[3]
    groups = kv_width // HEAD
    rows = summary_q.shape[0]
    tile_rows = rows // tile_num
    repeat = summary_q.shape[1] // kv_width
    col_cap = max(2, -(-(tile_num * list_len) // shards))
    req_devs = REQ_TILES // tile_num
    entries = tile_blocks.reshape(-1)
    live_mask = (jnp.arange(list_len, dtype=jnp.int32)[None, :] < tile_count[:, None]).reshape(-1)
    block_ids = jnp.arange(block_slot.shape[0], dtype=jnp.int32)
    stored_at = jnp.sum(
        jnp.where(entries[:, None] == block_ids[None, :], block_slot[None, :], 0), axis=1
    )
    owner_dev = stored_at // blk_dev
    local_slot = stored_at % blk_dev
    requests, position = request_table(
        owner_dev % shards, live_mask, shards, col_cap, owner_dev // shards * blk_dev + local_slot
    )
    wanted = jnp.maximum(lax.all_to_all(requests, "ctx", split_axis=0, concat_axis=0, tiled=True), 0)
    position = jnp.where(live_mask, position, 0)
    own = summary_kv.reshape(rows, 2 * kv_width)
    half_width = kv_width // HALVES
    slots = min(shards - 1, STAGES)
    state = (groups, tile_num, repeat * tile_rows)
    vmem, smem = pl.BlockSpec(memory_space=pltpu.VMEM), pl.BlockSpec(memory_space=pltpu.SMEM)
    dma = pltpu.SemaphoreType.DMA
    return pl.pallas_call(
        functools.partial(join, planes, shards, col_cap),
        out_shape=jax.ShapeDtypeStruct(summary_q.shape, jnp.bfloat16),
        in_specs=[smem] * 3 + [vmem] * 3,
        out_specs=vmem,
        scratch_shapes=[
            pltpu.VMEM((req_devs - 1, rows, 2 * kv_width), jnp.bfloat16),
            pltpu.VMEM((rows, 2 * kv_width), jnp.bfloat16),
            (pltpu.VMEM((planes * blk_dev, 2, block_len, half_width), jnp.bfloat16),) * HALVES,
            pltpu.VMEM((HALVES, slots, col_cap, 2, block_len, half_width), jnp.bfloat16),
            (pltpu.VMEM((shards * col_cap, 2, block_len, half_width), jnp.bfloat16),) * HALVES,
            pltpu.VMEM(state + (HEAD,), jnp.float32),
            pltpu.VMEM(state + (2 * HEAD,), jnp.float32),
            dma((req_devs - 1,)),
            dma((req_devs - 1,)),
            dma((2,)),
            dma,
            dma((HALVES, planes - 1)),
            dma((HALVES, planes - 1)),
            dma((HALVES, slots)),
            dma((HALVES, shards - 1)),
        ],
        compiler_params=pltpu.CompilerParams(
            collective_id=0, has_side_effects=True, vmem_limit_bytes=62 * 2**20
        ),
    )(wanted.reshape(-1), position, tile_count, summary_q, own, kv_cache)


def solution(mesh):
    in_specs = (
        P(("branch", "ctx"), None),
        P(("branch", "ctx"), None, None),
        P(("branch", "ctx"), None, None, None),
        P(),
        P(("branch", "ctx"), None),
        P(("branch", "ctx")),
    )
    out_specs = P(("branch", "ctx"), None)
    return jax.shard_map(local, mesh=mesh, in_specs=in_specs, out_specs=out_specs, check_vma=False)
```

time: 320 us -> 171 us (0.53)
  the two profiles are of different devices: /device:TPU:8 before, /device:TPU:15 now
where the time goes in v2:
time: 171 us
  Pallas kernels  156 us (91%)
  local copies, waits for them, and re-layouts  8.03 us (5%)
  starting transfers between devices  4.51 us (3%)
  other arithmetic  2.52 us (1%)
    pallas_call x1, Pallas kernels, local(): pl.pallas_call(functools.partial(join, planes, shards, col_cap), out_shap...  156 us
    unnamed x2, local copies, waits for them, and re-layouts  5.84 us
    all_to_all x1, starting transfers between devices, local(): lax.all_to_all(requests, 'ctx', split_axis=0, concat_axis=0, tiled=True)  4.51 us
  transfers between devices with their start and end apart: 1, of which 0 were waited for; matrix products, arithmetic and copies ran while one was open for 1% of the time, Pallas kernels for 0%

profile of v2, /device:TPU:15, one launch (start us, length us, event | category | flops | bytes accessed | tf_op | source)
XLA Modules:
  0.0 170.9 jit_solution(16274828726504259046)
XLA Ops:
  0.0 0.8 eq.44
  0.8 0.7 iota_compare_fusion.3
  1.5 0.1 lt.37
  1.6 0.8 select_reduce_fusion.2
  2.4 0.1 fusion.1
  2.6 0.2 select_reduce_fusion.1
  2.7 0.5 broadcast_select_fusion.1
  3.3 0.1 select_reduce_fusion
  3.4 0.7 all_to_all.6
  4.0 4.5 %all-to-all-start = ((s32[8,1,2]{2,1,0:T(1,128)}), s32[8,1,2]{2,1,0:T(1,128)S(1)}, u32[]{:S(2)}, u32[]{:S(2)}) async-start(s32[8,1,2]{2,1,0:T(1,128)} %bitcast), calls=%async_computation | async-start | bytes 8192 | tf_op jit(solution)/shard_map/all_to_all | solution.py:283
  8.5 2.4 %copy.9 = bf16[64,8,2,512]{3,1,2,0:T(8,128)(2,1)} copy(bf16[64,8,2,512]{3,2,1,0:T(2,128)(2,1)} %bitcast.4) | data formatting | bytes 2097152
  11.0 0.0 all-to-all-done
  11.0 0.7 max.8.wanted
  11.7 155.8 %shard_map.64 = bf16[512,2560]{1,0:T(8,128)(2,1)} custom-call(s32[16]{0:T(128)} %max.8.wanted, s32[16]{0:T(128)} %get-tuple-element.7.position, s32[4]{0:T(128)} %count.1, bf16[512,2560]{1,0:T(8,128)(2,1)} %q_ref.1, bf16[512,1024]{1,0:T(8,128)(2,1)} %bitcast.3, bf16[4,2,128,512]{3,2,1,0:T(8,128)(2,1)} %cache.1), custom_call_target="tpu_custom_call" | custom-call | tf_op jit(solution)/shard_map/pallas_call | solution.py:291
  167.5 3.4 %copy.11 = bf16[512,2560]{1,0:T(8,128)(2,1)} copy(bf16[512,2560]{1,0:T(8,128)(2,1)} %shard_map.64) | data formatting | bytes 5242880
  (3 shorter events, 0.1 us)
Async XLA Ops:
  4.0 7.0 %all-to-all-start = ((s32[8,1,2]{2,1,0:T(1,128)}), s32[8,1,2]{2,1,0:T(1,128)S(1)}, u32[]{:S(2)}, u32[]{:S(2)}) async-start(s32[8,1,2]{2,1,0:T(1,128)} %bitcast), calls=%async_computation | async-start | bytes 8192 | tf_op jit(solution)/shard_map/all_to_all | solution.py:283

commit v3 on v2

--- a/solution.py
+++ b/solution.py
@@ -138,9 +138,10 @@
 
 def join(
     planes, shards, capacity,
-    wanted, position, count, q_ref, own, cache, o_ref,
-    earlier, relay, column, payload, received, top, acc,
-    kv_send, kv_recv, hop_sem, fwd_send, gather_send, gather_recv, list_send, list_recv,
+    position, count, requests, q_ref, own, cache, o_ref,
+    earlier, relay, column, payload, received, top, acc, arrived, wanted,
+    kv_send, kv_recv, side_send, hop_sem, fwd_send, gather_send, gather_recv, list_send, list_recv,
+    ask_send, ask_recv, ask_local,
 ):
     z, c = lax.axis_index("branch"), lax.axis_index("ctx")
     req_devs = earlier.shape[0] + 1
@@ -170,12 +171,25 @@
         pl.semaphore_signal(barrier, inc=1, device_id=line_peer(step), device_id_type=pl.DeviceIdType.MESH)
     pl.semaphore_wait(barrier, shards + planes - 2)
 
+    asks = []
+    for step in range(1, shards):
+        ask = remote(
+            requests.at[lax.rem(c + step, shards)], arrived.at[c],
+            ask_send.at[step - 1], ask_recv.at[step - 1], plane_peer(step),
+        )
+        ask.start()
+        asks.append(ask)
     hop = remote(own, relay, hop_sem.at[0], hop_sem.at[1], line_peer(1))
     pl.when(crosses)(hop.start)
     pushes = []
     for step in range(1, req_devs):
         push = remote(own, earlier.at[place], kv_send.at[step - 1], kv_recv.at[place], plane_peer(step))
         sends = jnp.logical_and(place + step < req_devs, c + step < shards)
+        if step % 2:
+            direct = place + step == req_devs - 1
+            if step == 1:
+                direct = jnp.logical_or(direct, lax.rem(c, 2) == 0)
+            sends = jnp.logical_and(sends, direct)
         pl.when(sends)(push.start)
         pushes.append((sends, push))
 
@@ -187,18 +201,42 @@
                 cache.at[:, :, :, lanes], column[half].at[pl.ds(z * blk_dev, blk_dev)],
                 gather_send.at[half, step - 1], gather_recv.at[half, step - 1], line_peer(step),
             )
-            copy.start()
+            if half == 0:
+                copy.start()
             gathers.append(copy)
     for half in range(HALVES):
         column[half][pl.ds(z * blk_dev, blk_dev)] = cache[:, :, :, half * half_width : (half + 1) * half_width]
 
     own_block(own, q_ref, top, acc)
 
+    odd = lax.rem(c, 2)
+    last = place == req_devs - 1
+    sibling = (z, c + 1 - 2 * odd)
+    near = lax.div(place, 2)
+
+    def hand_on(slot):
+        return remote(earlier.at[slot], earlier.at[slot], side_send.at[slot], kv_recv.at[slot], sibling)
+
     def absorb_earlier(step, carry):
-        slot = jnp.where(c == 0, step, place - 1 - step)
-        remote(earlier.at[slot], earlier.at[slot], kv_send.at[0], kv_recv.at[slot], plane_peer(1)).wait_recv()
+        k = step - odd
+        handed = place - 1 - odd * 2 - 2 * (k - near)
+        slot = jnp.where(k < near, place - 2 - 2 * k, handed)
+        slot = jnp.where(k < 0, place - 1, slot)
+        slot = jnp.where(last, step, slot)
+        copy = hand_on(slot)
+        copy.wait_recv()
+        straight = jnp.logical_and(jnp.logical_and(k >= 0, k < near), place < req_devs - 1)
+        pl.when(straight)(copy.start)
         earlier_block(earlier.at[slot], q_ref, top, acc)
         return carry
+
+    def ask_own():
+        for ask in asks:
+            ask.wait_recv()
+        arrived[c] = requests[c]
+        copy = pltpu.make_async_copy(arrived, wanted, ask_local)
+        copy.start()
+        copy.wait()
 
     def send_listed(half):
         for step in range(1, planes):
@@ -211,7 +249,7 @@
                 copies[step - slots - 1].wait_send()
             target = received[half].at[pl.ds(c * capacity, capacity)]
             for i in range(capacity):
-                block = column[half][wanted[to * capacity + i]]
+                block = column[half][wanted[to, 0, i]]
                 if step == 0:
                     received[half][c * capacity + i] = block
                 else:
@@ -225,9 +263,8 @@
                 copies.append(copy)
         return copies
 
-    first = jnp.minimum(place, 1)
-    later = jnp.minimum(place, req_devs - 3)
-    lax.fori_loop(0, first, absorb_earlier, 0)
+    marks = [jnp.minimum(place, n) for n in (1, req_devs - 4, req_devs - 3, req_devs - 2)]
+    lax.fori_loop(0, marks[0], absorb_earlier, 0)
     forward = remote(relay, earlier.at[place], fwd_send, kv_recv.at[place], (z, 0))
 
     @pl.when(crosses)
@@ -235,11 +272,18 @@
         hop.wait_recv()
         forward.start()
 
-    lax.fori_loop(first, later, absorb_earlier, 0)
+    lax.fori_loop(marks[0], marks[1], absorb_earlier, 0)
+    for copy in gathers[: planes - 1]:
+        copy.wait_send()
+    for copy in gathers[planes - 1 :]:
+        copy.start()
+    ask_own()
+    lax.fori_loop(marks[1], marks[2], absorb_earlier, 0)
     lists = [send_listed(0)]
-    lax.fori_loop(later, place, absorb_earlier, 0)
+    lax.fori_loop(marks[2], marks[3], absorb_earlier, 0)
     for half in range(1, HALVES):
         lists.append(send_listed(half))
+    lax.fori_loop(marks[3], place, absorb_earlier, 0)
     for half in range(HALVES):
         for copy in lists[half]:
             copy.wait_recv()
@@ -250,7 +294,10 @@
     pl.when(crosses)(forward.wait_send)
     for sends, push in pushes:
         pl.when(sends)(push.wait_send)
-    for copy in gathers:
+    for slot in range(req_devs - 1):
+        handed = jnp.logical_and(slot < place, lax.rem(place - slot, 2) == 0)
+        pl.when(jnp.logical_and(handed, place < req_devs - 1))(hand_on(slot).wait_send)
+    for copy in gathers[planes - 1 :] + asks:
         copy.wait_send()
     for copies in lists:
         for copy in copies[-slots:]:
@@ -280,7 +327,8 @@
     requests, position = request_table(
         owner_dev % shards, live_mask, shards, col_cap, owner_dev // shards * blk_dev + local_slot
     )
-    wanted = jnp.maximum(lax.all_to_all(requests, "ctx", split_axis=0, concat_axis=0, tiled=True), 0)
+    requests = jnp.pad(jnp.maximum(requests, 0), ((0, 0), (0, HEAD - col_cap)))
+    requests = jnp.broadcast_to(requests[:, None, :], (shards, 8, HEAD))
     position = jnp.where(live_mask, position, 0)
     own = summary_kv.reshape(rows, 2 * kv_width)
     half_width = kv_width // HALVES
@@ -291,7 +339,7 @@
     return pl.pallas_call(
         functools.partial(join, planes, shards, col_cap),
         out_shape=jax.ShapeDtypeStruct(summary_q.shape, jnp.bfloat16),
-        in_specs=[smem] * 3 + [vmem] * 3,
+        in_specs=[smem] * 2 + [vmem] * 4,
         out_specs=vmem,
         scratch_shapes=[
             pltpu.VMEM((req_devs - 1, rows, 2 * kv_width), jnp.bfloat16),
@@ -301,6 +349,9 @@
             (pltpu.VMEM((shards * col_cap, 2, block_len, half_width), jnp.bfloat16),) * HALVES,
             pltpu.VMEM(state + (HEAD,), jnp.float32),
             pltpu.VMEM(state + (2 * HEAD,), jnp.float32),
+            pltpu.VMEM((shards, 8, HEAD), jnp.int32),
+            pltpu.SMEM((shards, 8, HEAD), jnp.int32),
+            dma((req_devs - 1,)),
             dma((req_devs - 1,)),
             dma((req_devs - 1,)),
             dma((2,)),
@@ -309,11 +360,14 @@
             dma((HALVES, planes - 1)),
             dma((HALVES, slots)),
             dma((HALVES, shards - 1)),
+            dma((shards - 1,)),
+            dma((shards - 1,)),
+            dma,
         ],
         compiler_params=pltpu.CompilerParams(
             collective_id=0, has_side_effects=True, vmem_limit_bytes=62 * 2**20
         ),
-    )(wanted.reshape(-1), position, tile_count, summary_q, own, kv_cache)
+    )(position, tile_count, requests, summary_q, own, kv_cache)
 
 
 def solution(mesh):

time: 171 us -> 168 us (0.982)
  the two profiles are of different devices: /device:TPU:15 before, /device:TPU:21 now
where the time goes in v3:
time: 168 us
  Pallas kernels  158 us (94%)
  local copies, waits for them, and re-layouts  7.39 us (4%)
  other arithmetic  2.51 us (1%)
    pallas_call x1, Pallas kernels, local(): pl.pallas_call(functools.partial(join, planes, shards, col_cap), out_shap...  158 us
    unnamed x2, local copies, waits for them, and re-layouts  5.84 us

profile of v3, /device:TPU:21, one launch (start us, length us, event | category | flops | bytes accessed | tf_op | source)
XLA Modules:
  0.0 167.9 jit_solution(10959443590527741997)
XLA Ops:
  0.0 0.8 eq.44
  0.8 0.8 select_reduce_fusion.2
  1.6 0.7 iota_compare_fusion.3
  2.3 0.1 lt.37
  2.5 0.1 fusion.1
  2.6 0.2 select_reduce_fusion.1
  2.8 0.5 broadcast_select_fusion
  3.3 0.1 select_reduce_fusion
  3.4 0.1 max.7
  3.5 0.6 broadcast_in_dim.46.requests
  4.1 2.4 %copy.7 = bf16[64,8,2,512]{3,1,2,0:T(8,128)(2,1)} copy(bf16[64,8,2,512]{3,2,1,0:T(2,128)(2,1)} %bitcast.3) | data formatting | bytes 2097152
  6.5 158.0 %shard_map.64 = bf16[512,2560]{1,0:T(8,128)(2,1)} custom-call(s32[16]{0:T(128)} %get-tuple-element.8.position, s32[4]{0:T(128)} %count.1, s32[8,8,128]{2,1,0:T(8,128)} %broadcast_in_dim.46.requests, bf16[512,2560]{1,0:T(8,128)(2,1)} %q_ref.1, bf16[512,1024]{1,0:T(8,128)(2,1)} %bitcast.2, bf16[4,2,128,512]{3,2,1,0:T(8,128)(2,1)} %cache.1), custom_call_target="tpu_custom_call" | custom-call | tf_op jit(solution)/shard_map/pallas_call | solution.py:339
  164.5 3.4 %copy.9 = bf16[512,2560]{1,0:T(8,128)(2,1)} copy(bf16[512,2560]{1,0:T(8,128)(2,1)} %shard_map.64) | data formatting | bytes 5242880
  (5 shorter events, 0.1 us)

commit v4 on v3

--- a/solution.py
+++ b/solution.py
@@ -71,15 +71,16 @@
 def own_block(own, q_ref, top, acc):
     groups, tile_num = acc.shape[:2]
     tile_rows = own.shape[0] // tile_num
-    shape = (acc.shape[2], own.shape[0])
-    query_row = lax.rem(lax.broadcasted_iota(jnp.int32, shape, 0), tile_rows)
-    key_row = lax.broadcasted_iota(jnp.int32, shape, 1)
 
     def body(group, carry):
         keys, values = own[:, head_lanes(group)], own[:, head_lanes(groups + group)]
         for tile in range(tile_num):
+            seen = (tile + 1) * tile_rows
+            shape = (acc.shape[2], seen)
+            query_row = lax.rem(lax.broadcasted_iota(jnp.int32, shape, 0), tile_rows)
+            key_row = lax.broadcasted_iota(jnp.int32, shape, 1)
             mask = key_row <= query_row + tile * tile_rows
-            absorb(group, tile, keys, values, mask, True, q_ref, top, acc)
+            absorb(group, tile, keys[:seen], values[:seen], mask, True, q_ref, top, acc)
         return carry
 
     lax.fori_loop(0, groups, body, 0)
@@ -201,8 +202,7 @@
                 cache.at[:, :, :, lanes], column[half].at[pl.ds(z * blk_dev, blk_dev)],
                 gather_send.at[half, step - 1], gather_recv.at[half, step - 1], line_peer(step),
             )
-            if half == 0:
-                copy.start()
+            copy.start()
             gathers.append(copy)
     for half in range(HALVES):
         column[half][pl.ds(z * blk_dev, blk_dev)] = cache[:, :, :, half * half_width : (half + 1) * half_width]
@@ -263,7 +263,7 @@
                 copies.append(copy)
         return copies
 
-    marks = [jnp.minimum(place, n) for n in (1, req_devs - 4, req_devs - 3, req_devs - 2)]
+    marks = [jnp.minimum(place, n) for n in (1, req_devs - 5, req_devs - 3)]
     lax.fori_loop(0, marks[0], absorb_earlier, 0)
     forward = remote(relay, earlier.at[place], fwd_send, kv_recv.at[place], (z, 0))
 
@@ -273,21 +273,19 @@
         forward.start()
 
     lax.fori_loop(marks[0], marks[1], absorb_earlier, 0)
-    for copy in gathers[: planes - 1]:
-        copy.wait_send()
-    for copy in gathers[planes - 1 :]:
-        copy.start()
     ask_own()
+    lists = [send_listed(0)]
     lax.fori_loop(marks[1], marks[2], absorb_earlier, 0)
-    lists = [send_listed(0)]
-    lax.fori_loop(marks[2], marks[3], absorb_earlier, 0)
-    for half in range(1, HALVES):
-        lists.append(send_listed(half))
-    lax.fori_loop(marks[3], place, absorb_earlier, 0)
-    for half in range(HALVES):
+    lists.append(send_listed(1))
+
+    def absorb_listed(half):
         for copy in lists[half]:
             copy.wait_recv()
         branch_blocks(half, position, count, received[half], q_ref, top, acc)
+
+    absorb_listed(0)
+    lax.fori_loop(marks[2], place, absorb_earlier, 0)
+    absorb_listed(1)
     store_result(o_ref, acc)
 
     pl.when(crosses)(hop.wait_send)
@@ -297,7 +295,7 @@
     for slot in range(req_devs - 1):
         handed = jnp.logical_and(slot < place, lax.rem(place - slot, 2) == 0)
         pl.when(jnp.logical_and(handed, place < req_devs - 1))(hand_on(slot).wait_send)
-    for copy in gathers[planes - 1 :] + asks:
+    for copy in gathers + asks:
         copy.wait_send()
     for copies in lists:
         for copy in copies[-slots:]:

time: 168 us -> 162 us (0.964)
  the two profiles are of different devices: /device:TPU:21 before, /device:TPU:9 now
where the time goes in v4:
time: 162 us; the launch traced here: 161 us
  Pallas kernels  151 us (93%)
  local copies, waits for them, and re-layouts  7.39 us (5%)
  other arithmetic  2.51 us (2%)
    pallas_call x1, Pallas kernels, local(): pl.pallas_call(functools.partial(join, planes, shards, col_cap), out_shap...  151 us
    unnamed x2, local copies, waits for them, and re-layouts  5.84 us

profile of v4, /device:TPU:9, one launch (start us, length us, event | category | flops | bytes accessed | tf_op | source)
XLA Modules:
  0.0 161.3 jit_solution(2984079818552963713)
XLA Ops:
  0.0 0.8 eq.44
  0.8 0.8 select_reduce_fusion.2
  1.6 0.7 iota_compare_fusion.3
  2.3 0.1 lt.37
  2.5 0.1 fusion.1
  2.6 0.2 select_reduce_fusion.1
  2.8 0.5 broadcast_select_fusion
  3.3 0.1 select_reduce_fusion
  3.4 0.1 max.7
  3.5 0.6 broadcast_in_dim.46.requests
  4.1 2.4 %copy.7 = bf16[64,8,2,512]{3,1,2,0:T(8,128)(2,1)} copy(bf16[64,8,2,512]{3,2,1,0:T(2,128)(2,1)} %bitcast.3) | data formatting | bytes 2097152
  6.5 151.4 %shard_map.64 = bf16[512,2560]{1,0:T(8,128)(2,1)} custom-call(s32[16]{0:T(128)} %get-tuple-element.8.position, s32[4]{0:T(128)} %count.1, s32[8,8,128]{2,1,0:T(8,128)} %broadcast_in_dim.46.requests, bf16[512,2560]{1,0:T(8,128)(2,1)} %q_ref.1, bf16[512,1024]{1,0:T(8,128)(2,1)} %bitcast.2, bf16[4,2,128,512]{3,2,1,0:T(8,128)(2,1)} %cache.1), custom_call_target="tpu_custom_call" | custom-call | tf_op jit(solution)/shard_map/pallas_call | solution.py:337
  157.9 3.4 %copy.9 = bf16[512,2560]{1,0:T(8,128)(2,1)} copy(bf16[512,2560]{1,0:T(8,128)(2,1)} %shard_map.64) | data formatting | bytes 5242880
  (5 shorter events, 0.1 us)

commit v5 on v4

--- a/solution.py
+++ b/solution.py
@@ -202,7 +202,8 @@
                 cache.at[:, :, :, lanes], column[half].at[pl.ds(z * blk_dev, blk_dev)],
                 gather_send.at[half, step - 1], gather_recv.at[half, step - 1], line_peer(step),
             )
-            copy.start()
+            if half == 0:
+                copy.start()
             gathers.append(copy)
     for half in range(HALVES):
         column[half][pl.ds(z * blk_dev, blk_dev)] = cache[:, :, :, half * half_width : (half + 1) * half_width]
@@ -263,7 +264,7 @@
                 copies.append(copy)
         return copies
 
-    marks = [jnp.minimum(place, n) for n in (1, req_devs - 5, req_devs - 3)]
+    marks = [jnp.minimum(place, n) for n in (1, 2, req_devs - 5, req_devs - 3)]
     lax.fori_loop(0, marks[0], absorb_earlier, 0)
     forward = remote(relay, earlier.at[place], fwd_send, kv_recv.at[place], (z, 0))
 
@@ -273,9 +274,14 @@
         forward.start()
 
     lax.fori_loop(marks[0], marks[1], absorb_earlier, 0)
+    for copy in gathers[: planes - 1]:
+        copy.wait_send()
+    for copy in gathers[planes - 1 :]:
+        copy.start()
+    lax.fori_loop(marks[1], marks[2], absorb_earlier, 0)
     ask_own()
     lists = [send_listed(0)]
-    lax.fori_loop(marks[1], marks[2], absorb_earlier, 0)
+    lax.fori_loop(marks[2], marks[3], absorb_earlier, 0)
     lists.append(send_listed(1))
 
     def absorb_listed(half):
@@ -284,7 +290,7 @@
         branch_blocks(half, position, count, received[half], q_ref, top, acc)
 
     absorb_listed(0)
-    lax.fori_loop(marks[2], place, absorb_earlier, 0)
+    lax.fori_loop(marks[3], place, absorb_earlier, 0)
     absorb_listed(1)
     store_result(o_ref, acc)
 
@@ -295,7 +301,7 @@
     for slot in range(req_devs - 1):
         handed = jnp.logical_and(slot < place, lax.rem(place - slot, 2) == 0)
         pl.when(jnp.logical_and(handed, place < req_devs - 1))(hand_on(slot).wait_send)
-    for copy in gathers + asks:
+    for copy in gathers[planes - 1 :] + asks:
         copy.wait_send()
     for copies in lists:
         for copy in copies[-slots:]:

time: 162 us -> 168 us (1.037)
  the two profiles are of different devices: /device:TPU:9 before, /device:TPU:17 now
where the time goes in v5:
time: 168 us
  Pallas kernels  158 us (94%)
  local copies, waits for them, and re-layouts  7.39 us (4%)
  other arithmetic  2.51 us (1%)
    pallas_call x1, Pallas kernels, local(): pl.pallas_call(functools.partial(join, planes, shards, col_cap), out_shap...  158 us
    unnamed x2, local copies, waits for them, and re-layouts  5.84 us

profile of v5, /device:TPU:17, one launch (start us, length us, event | category | flops | bytes accessed | tf_op | source)
XLA Modules:
  0.0 168.3 jit_solution(8474430694864315402)
XLA Ops:
  0.0 0.8 eq.44
  0.8 0.8 select_reduce_fusion.2
  1.6 0.7 iota_compare_fusion.3
  2.3 0.1 lt.37
  2.5 0.1 fusion.1
  2.6 0.2 select_reduce_fusion.1
  2.8 0.5 broadcast_select_fusion
  3.3 0.1 select_reduce_fusion
  3.4 0.1 max.7
  3.5 0.6 broadcast_in_dim.46.requests
  4.1 2.4 %copy.7 = bf16[64,8,2,512]{3,1,2,0:T(8,128)(2,1)} copy(bf16[64,8,2,512]{3,2,1,0:T(2,128)(2,1)} %bitcast.3) | data formatting | bytes 2097152
  6.5 158.3 %shard_map.64 = bf16[512,2560]{1,0:T(8,128)(2,1)} custom-call(s32[16]{0:T(128)} %get-tuple-element.8.position, s32[4]{0:T(128)} %count.1, s32[8,8,128]{2,1,0:T(8,128)} %broadcast_in_dim.46.requests, bf16[512,2560]{1,0:T(8,128)(2,1)} %q_ref.1, bf16[512,1024]{1,0:T(8,128)(2,1)} %bitcast.2, bf16[4,2,128,512]{3,2,1,0:T(8,128)(2,1)} %cache.1), custom_call_target="tpu_custom_call" | custom-call | tf_op jit(solution)/shard_map/pallas_call | solution.py:343
  164.9 3.4 %copy.9 = bf16[512,2560]{1,0:T(8,128)(2,1)} copy(bf16[512,2560]{1,0:T(8,128)(2,1)} %shard_map.64) | data formatting | bytes 5242880
  (5 shorter events, 0.1 us)
